TPU v7x, 512 devices: a whole 4x8x8 slice. The times are simulated.
512 devices in a mesh: wa: 64 (over y, x, z_hi), gz: 8 (over z_lo, core).
Axes of the slice: x: 4, y: 8, z: 8 (z_hi: 2, z_lo: 4; z = z_hi * 4 + z_lo), core: 2. Of those that a mesh axis runs over, the one named last changes fastest.
Arguments:
- wave: float32 [2, 8, 2048, 2048], P(None, 'gz', 'wa'), may hold values from -6 to 6
- potential: float32 [8, 2048, 2048], P('gz', 'wa'), may hold values from 0 to 800
Outputs:
- evolved: float32 [2, 8, 2048, 2048], P(None, 'gz', 'wa')
All inputs are finite; a program needn't handle non-finite values.
Results may differ from a plain program's by a relative error of at most 0.0083.
Values may be sent and summed in bfloat16 or wider, within the bound.
No kernel may reach another device: no remote copies, remote signals or barrier semaphores. Data moves between devices by JAX's collectives and lax.ppermute only.
A program may use at most 64 MiB of HBM per device.

v0:
```python
import math

import jax
import jax.numpy as jnp
import numpy as np
from jax import lax
from jax.experimental import pallas as pl
from jax.experimental.pallas import tpu as pltpu
from jax.sharding import PartitionSpec as P

time_step = 0.001
spacing = 1.0 / 32.0
rotation = 0.9
coupling = 400.0
z_coupling = 0.25

GRID = 2048
LANES = 128
COLS = 16
ROWS = 32
GROUPS = 4
PARTS_WA = 64

NEAR = (2.0 * z_coupling * z_coupling, z_coupling)
FAR = -0.5 * z_coupling * z_coupling
CENTRE = (1.0 - 3.0 * z_coupling * z_coupling, -2.0 * z_coupling)
CENTRE_EDGE = 1.0 - 2.5 * z_coupling * z_coupling


def tables():
    lane = np.arange(LANES)
    turned_lane = 32 * ((lane // 8) % 4) + 8 * (lane // 32) + lane % 8
    scale = 1.0 / math.sqrt(GRID)

    def matrices(order):
        angle = 2.0 * np.pi * ((order[:, None] * lane[None, :]) % LANES) / LANES
        cos, sin = np.cos(angle) * scale, np.sin(angle) * scale
        forward = np.block([[cos, -sin], [sin, cos]])
        return forward

    def split(matrix):
        high = matrix.astype(jnp.bfloat16)
        low = (matrix - high.astype(np.float64)).astype(jnp.bfloat16)
        return np.stack([np.asarray(high), np.asarray(low)])

    def twiddle(order):
        angle = 2.0 * np.pi * np.arange(COLS)[:, None] * order[None, :] / GRID
        return np.stack([np.cos(angle), np.sin(angle)]).astype(np.float32)

    angle = 2.0 * np.pi * ((lane[:, None] * lane[None, :]) % LANES) / LANES
    cos, sin = np.cos(angle) * scale, np.sin(angle) * scale
    backward = split(np.block([[cos, sin], [-sin, cos]]))
    mode = np.arange(COLS)[:, None] + COLS * lane[None, :]
    signed = np.where(mode < GRID // 2, mode, mode - GRID).astype(np.float64)
    wavenum = signed * (2.0 * np.pi / (GRID * spacing))
    slope = time_step * rotation * spacing * wavenum
    rows8 = slope[:, None, :] * np.arange(8)[None, :, None]
    own = np.stack([np.cos(rows8), np.sin(rows8)]).astype(np.float32)
    step8 = np.stack([np.cos(8.0 * slope), np.sin(8.0 * slope)]).astype(np.float32)
    return {
        "fwd_x": split(matrices(lane)),
        "fwd_y": split(matrices(turned_lane)),
        "inv": backward,
        "tw_x": twiddle(lane),
        "tw_y": twiddle(turned_lane),
        "wavenum": wavenum.astype(np.float32),
        "own": own,
        "step8": step8,
    }


def sincos(angle):
    turns = jnp.floor(angle * (2.0 / math.pi) + 0.5)
    rest = angle - turns * 1.5703125
    rest = rest - turns * 4.837512969970703e-4
    rest = rest - turns * 7.54978995489188e-8
    square = rest * rest
    sine = rest + rest * square * (
        -1.6666654611e-1 + square * (8.3321608736e-3 - square * 1.9515295891e-4)
    )
    cosine = 1.0 - 0.5 * square + square * square * (
        4.166664568298827e-2 + square * (-1.388731625493765e-3 + square * 2.443315711809948e-5)
    )
    quadrant = turns.astype(jnp.int32)
    swapped = (quadrant & 1) == 1
    sin_out = jnp.where(swapped, cosine, sine)
    cos_out = jnp.where(swapped, sine, cosine)
    sin_out = jnp.where((quadrant & 2) == 2, -sin_out, sin_out)
    cos_out = jnp.where(((quadrant + 1) & 2) == 2, -cos_out, cos_out)
    return sin_out, cos_out


def dft4(v, sign):
    (ar, ai), (br, bi), (cr, ci), (dr, di) = v
    sr, si, tr, ti = ar + cr, ai + ci, ar - cr, ai - ci
    ur, ui, wr, wi = br + dr, bi + di, br - dr, bi - di
    if sign > 0:
        p, q = (tr + wi, ti - wr), (tr - wi, ti + wr)
    else:
        p, q = (tr - wi, ti + wr), (tr + wi, ti - wr)
    return [(sr + ur, si + ui), p, (sr - ur, si - ui), q]


def turn16(v, power, sign):
    power %= 16
    re, im = v
    if power == 0:
        return v
    c, s = math.cos(2.0 * math.pi * power / 16), -sign * math.sin(2.0 * math.pi * power / 16)
    if power == 4:
        return (im, -re) if sign > 0 else (-im, re)
    if power % 2 == 0:
        h = math.sqrt(0.5)
        return (h * (_pm(re, c) + _pm(im, -s)), h * (_pm(re, s) + _pm(im, c)))
    return (re * c - im * s, re * s + im * c)


def _pm(x, sign):
    return x if sign > 0 else -x


def dft16(v, sign):
    low = [dft4([v[4 * a + b] for a in range(4)], sign) for b in range(4)]
    out = [None] * 16
    for k in range(4):
        high = dft4([turn16(low[b][k], b * k, sign) for b in range(4)], sign)
        for k2 in range(4):
            out[k + 4 * k2] = high[k2]
    return out


def swap_blocks(v):
    lane = lax.broadcasted_iota(jnp.int32, (8, LANES), 1)

    def stage(first, second, width):
        upper = (lane // width) % 2 == 1
        a = jnp.where(upper, pltpu.roll(second, width, 1), first)
        b = jnp.where(upper, second, pltpu.roll(first, LANES - width, 1))
        return a, b

    v0, v2 = stage(v[0], v[2], 64)
    v1, v3 = stage(v[1], v[3], 64)
    v0, v1 = stage(v0, v1, 32)
    v2, v3 = stage(v2, v3, 32)
    return [v0, v1, v2, v3]


def row_phases(first_row, wavenum, step8, sign):
    angle = time_step * (0.5 * wavenum * wavenum + (sign * rotation * first_row) * wavenum)
    sine, cosine = sincos(angle)
    re, im = cosine, -sine
    sr, si = step8[0], -sign * step8[1]
    out = [(re, im)]
    for _ in range(GROUPS - 1):
        re, im = re * sr - im * si, re * si + im * sr
        out.append((re, im))
    return out


def double_dot(left, table_ref):
    return jnp.dot(left, table_ref[0], preferred_element_type=jnp.float32) + jnp.dot(
        left, table_ref[1], preferred_element_type=jnp.float32
    )


def sweep(load, store, first_row, fwd_ref, inv_ref, tw_f_ref, tw_i_ref, wave_ref, own_ref, step_ref, buf, sign):
    for g in range(GROUPS):
        rows = slice(8 * g, 8 * g + 8)
        out = dft16([load(g, c) for c in range(COLS)], 1)
        for m in range(COLS):
            re, im = out[m]
            if m > 0:
                c, s = tw_f_ref[0, m : m + 1, :], tw_f_ref[1, m : m + 1, :]
                re, im = re * c + im * s, im * c - re * s
            buf[m, rows, :LANES] = re
            buf[m, rows, LANES:] = im
    spectrum = double_dot(buf[...].reshape(COLS * ROWS, 2 * LANES).astype(jnp.bfloat16), fwd_ref)
    buf[...] = spectrum.reshape(COLS, ROWS, 2 * LANES)
    phases = row_phases(first_row, wave_ref[...], step_ref[...], sign)
    for m in range(COLS):
        own_re, own_im = own_ref[0, m], -sign * own_ref[1, m]
        for g in range(GROUPS):
            rows = slice(8 * g, 8 * g + 8)
            row_re, row_im = phases[g][0][m : m + 1, :], phases[g][1][m : m + 1, :]
            f_re, f_im = own_re * row_re - own_im * row_im, own_re * row_im + own_im * row_re
            re, im = buf[m, rows, :LANES], buf[m, rows, LANES:]
            buf[m, rows, :LANES] = re * f_re - im * f_im
            buf[m, rows, LANES:] = re * f_im + im * f_re
    turned = double_dot(buf[...].reshape(COLS * ROWS, 2 * LANES).astype(jnp.bfloat16), inv_ref)
    buf[...] = turned.reshape(COLS, ROWS, 2 * LANES)
    for g in range(GROUPS):
        rows = slice(8 * g, 8 * g + 8)
        terms = []
        for m in range(COLS):
            re, im = buf[m, rows, :LANES], buf[m, rows, LANES:]
            if m > 0:
                c, s = tw_i_ref[0, m : m + 1, :], tw_i_ref[1, m : m + 1, :]
                re, im = re * c - im * s, im * c + re * s
            terms.append((re, im))
        for c, (re, im) in enumerate(dft16(terms, -1)):
            store(g, c, re, im)


def potential_kernel(wave_ref, potential_ref, out_ref):
    for g in range(2):
        rows = slice(16 * g, 16 * g + 16)
        for c in range(COLS):
            at = slice(LANES * c, LANES * c + LANES)
            re, im, pot = wave_ref[0, 0, rows, at], wave_ref[1, 0, rows, at], potential_ref[0, rows, at]
            sine, cosine = sincos(time_step * (pot + coupling * (re * re + im * im)))
            out_ref[0, rows, at] = (re * cosine + im * sine).astype(jnp.bfloat16)
            out_ref[1, rows, at] = (im * cosine - re * sine).astype(jnp.bfloat16)


def x_kernel(scalar_ref, own_ref, pair_ref, left_ref, right_ref, fwd_ref, inv_ref, tw_ref, wave_ref, rows_ref, step_ref, out_ref, mixed, buf, swept):
    centre = scalar_ref[1]
    for g in range(2):
        rows = slice(16 * g, 16 * g + 16)
        for c in range(COLS):
            at = slice(LANES * c, LANES * c + LANES)
            re, im, pre, pim, lre, lim, rre, rim = (
                ref[p, rows, at].astype(jnp.float32)
                for ref in (own_ref, pair_ref, left_ref, right_ref)
                for p in range(2)
            )
            mixed[0, rows, at] = centre * re - CENTRE[1] * im + (NEAR[0] * pre - NEAR[1] * pim) + (lre + rre)
            mixed[1, rows, at] = centre * im + CENTRE[1] * re + (NEAR[0] * pim + NEAR[1] * pre) + (lim + rim)

    def load(g, c):
        at = slice(LANES * c, LANES * c + LANES)
        return mixed[0, 8 * g : 8 * g + 8, at], mixed[1, 8 * g : 8 * g + 8, at]

    def store(g, c, re, im):
        swept[c, 0, g] = re
        swept[c, 1, g] = im

    sweep(load, store, scalar_ref[0], fwd_ref, inv_ref, tw_ref, tw_ref, wave_ref, rows_ref, step_ref, buf, 1.0)
    for c in range(COLS):
        re = swap_blocks([swept[c, 0, g] for g in range(GROUPS)])
        im = swap_blocks([swept[c, 1, g] for g in range(GROUPS)])
        for q in range(4):
            out_ref[4 * c + q] = jnp.concatenate([re[q], im[q]], axis=0).astype(jnp.bfloat16)


def y_kernel(scalar_ref, in_ref, fwd_ref, inv_ref, tw_f_ref, tw_i_ref, wave_ref, rows_ref, step_ref, out_ref, field, buf):
    for s in range(4):
        block = in_ref[16 * s : 16 * s + 16].astype(jnp.float32)
        for p in range(2):
            flipped = jnp.transpose(block[:, 8 * p : 8 * p + 8, :].reshape(LANES, LANES))
            for x in range(4):
                parts = swap_blocks([flipped[32 * g + 8 * x : 32 * g + 8 * x + 8] for g in range(4)])
                for a in range(4):
                    field[p, 8 * x : 8 * x + 8, LANES * (4 * s + a) : LANES * (4 * s + a + 1)] = parts[a]

    def load(g, c):
        at = slice(LANES * c, LANES * c + LANES)
        return field[0, 8 * g : 8 * g + 8, at], field[1, 8 * g : 8 * g + 8, at]

    def store(g, c, re, im):
        at = slice(LANES * c, LANES * c + LANES)
        out_ref[0, 0, 8 * g : 8 * g + 8, at] = re
        out_ref[1, 0, 8 * g : 8 * g + 8, at] = im

    sweep(load, store, scalar_ref[0], fwd_ref, inv_ref, tw_f_ref, tw_i_ref, wave_ref, rows_ref, step_ref, buf, -1.0)


SMEM = pl.BlockSpec(memory_space=pltpu.SMEM)
VMEM = pl.BlockSpec(memory_space=pltpu.VMEM)
PARAMS = pltpu.CompilerParams(vmem_limit_bytes=48 * 1024 * 1024)


def on_device(wave, potential):
    t = tables()
    f32, bf16 = jnp.float32, jnp.bfloat16
    row_base = lax.axis_index("wa") * ROWS - GRID // 2
    plane = lax.axis_index("gz")
    edge = (plane == 0) | (plane == 7)
    odd = (plane % 2).astype(f32)
    scalars = jnp.stack([row_base.astype(f32) * spacing, jnp.where(edge, CENTRE_EDGE, CENTRE[0])])
    own = pl.pallas_call(
        potential_kernel,
        out_shape=jax.ShapeDtypeStruct((2, ROWS, GRID), bf16),
        in_specs=[VMEM, VMEM],
        out_specs=VMEM,
        compiler_params=PARAMS,
    )(wave, potential)
    pair = lax.ppermute(own, "gz", [(i, i ^ 1) for i in range(8)])
    far = FAR * own.astype(f32)
    pr, pi = pair[0].astype(f32), pair[1].astype(f32)
    near = jnp.stack([NEAR[0] * pr - NEAR[1] * pi, NEAR[0] * pi + NEAR[1] * pr])
    to_right = (far + (1.0 - odd) * near).astype(bf16)
    to_left = (far + odd * near).astype(bf16)
    left = lax.ppermute(to_right, "gz", [(i, i + 2) for i in range(6)])
    right = lax.ppermute(to_left, "gz", [(i + 2, i) for i in range(6)])
    chunks = pl.pallas_call(
        x_kernel,
        out_shape=jax.ShapeDtypeStruct((PARTS_WA, 16, LANES), bf16),
        in_specs=[SMEM] + [VMEM] * 10,
        out_specs=VMEM,
        scratch_shapes=[
            pltpu.VMEM((2, ROWS, GRID), f32),
            pltpu.VMEM((COLS, ROWS, 2 * LANES), f32),
            pltpu.VMEM((COLS, 2, GROUPS, 8, LANES), f32),
        ],
        compiler_params=PARAMS,
    )(scalars, own, pair, left, right, t["fwd_x"], t["inv"], t["tw_x"], t["wavenum"], t["own"], t["step8"])
    chunks = lax.all_to_all(chunks, "wa", 0, 0, tiled=True)
    return pl.pallas_call(
        y_kernel,
        out_shape=jax.ShapeDtypeStruct((2, 1, ROWS, GRID), f32),
        in_specs=[SMEM] + [VMEM] * 8,
        out_specs=VMEM,
        scratch_shapes=[
            pltpu.VMEM((2, ROWS, GRID), f32),
            pltpu.VMEM((COLS, ROWS, 2 * LANES), f32),
        ],
        compiler_params=PARAMS,
    )(scalars, chunks, t["fwd_y"], t["inv"], t["tw_y"], t["tw_x"], t["wavenum"], t["own"], t["step8"])


def solution(mesh):
    in_specs = (P(None, "gz", "wa", None), P("gz", "wa", None))
    out_specs = P(None, "gz", "wa", None)
    return jax.shard_map(
        on_device, mesh=mesh, in_specs=in_specs, out_specs=out_specs, check_vma=False
    )
```

profile of v0, /device:TPU:64, one launch (start us, length us, event | category | flops | bytes accessed | tf_op | source)
XLA Modules:
  0.0 57.4 jit_solution(12270247537775720016)
XLA Ops:
  0.0 1.0 %copy-done.1 = f32[2,1,32,2048]{3,2,1,0:T(8,128)S(1)} copy-done((f32[2,1,32,2048]{3,2,1,0:T(8,128)S(1)}, f32[2,1,32,2048]{3,2,1,0:T(8,128)}, u32[]{:S(2)}) %copy-start.1) | copy-done | bytes 524312
  1.0 0.9 %copy-done.4 = f32[1,32,2048]{2,1,0:T(8,128)S(1)} copy-done((f32[1,32,2048]{2,1,0:T(8,128)S(1)}, f32[1,32,2048]{2,1,0:T(8,128)}, u32[]{:S(2)}) %copy-start.4) | copy-done | bytes 262168
  2.0 0.5 shard_map.100.own_ref
  2.5 1.9 %collective-permute-start = (bf16[2,32,2048]{2,1,0:T(8,128)(2,1)S(1)}, bf16[2,32,2048]{2,1,0:T(8,128)(2,1)S(1)}, u32[]{:S(2)}, u32[]{:S(2)}) collective-permute-start(bf16[2,32,2048]{2,1,0:T(8,128)(2,1)S(1)} %shard_map.100.own_ref), channel_id=1, source_target_pairs={{0,1},{1,0},{2,3},{3,2},{4,5},{5,4},{6,7},{7,6},{8,9},{9,8},{10,11... | collective-permute-start | bytes 786440 | tf_op jit(solution)/shard_map/ppermute | solution.py:287
  4.4 1.5 %collective-permute-done.pair_ref = bf16[2,32,2048]{2,1,0:T(8,128)(2,1)S(1)} collective-permute-done((bf16[2,32,2048]{2,1,0:T(8,128)(2,1)S(1)}, bf16[2,32,2048]{2,1,0:T(8,128)(2,1)S(1)}, u32[]{:S(2)}, u32[]{:S(2)}) %collective-permute-start) | collective-permute-done | bytes 262176 | tf_op jit(solution)/shard_map/ppermute | solution.py:287
  5.9 0.1 fusion
  6.0 0.0 copy-start
  6.0 0.0 copy-start.2
  6.0 0.0 copy-start.3
  6.0 0.0 copy-start.7
  6.0 0.1 add_convert_fusion
  6.2 0.0 copy-start.6
  6.2 7.1 %collective-permute-start.2 = (bf16[2,32,2048]{2,1,0:T(8,128)(2,1)S(1)}, bf16[2,32,2048]{2,1,0:T(8,128)(2,1)S(1)}, u32[]{:S(2)}, u32[]{:S(2)}) collective-permute-start(bf16[2,32,2048]{2,1,0:T(8,128)(2,1)S(1)} %get-tuple-element.5), channel_id=1, source_target_pairs={{2,0},{3,1},{4,2},{5,3},{6,4},{7,5},{10,8},{11,9},{12,10},{13,11},... | collective-permute-start | bytes 786440 | tf_op jit(solution)/shard_map/ppermute | solution.py:294
  13.2 1.9 %collective-permute-start.1 = (bf16[2,32,2048]{2,1,0:T(8,128)(2,1)S(1)}, bf16[2,32,2048]{2,1,0:T(8,128)(2,1)S(1)}, u32[]{:S(2)}, u32[]{:S(2)}) collective-permute-start(bf16[2,32,2048]{2,1,0:T(8,128)(2,1)S(1)} %get-tuple-element.6), channel_id=1, source_target_pairs={{0,2},{1,3},{2,4},{3,5},{4,6},{5,7},{8,10},{9,11},{10,12},{11,13},... | collective-permute-start | bytes 786440 | tf_op jit(solution)/shard_map/ppermute | solution.py:293
  15.2 0.0 copy-start.8
  15.2 0.1 pad_maximum_fusion.1.scalar_ref
  15.3 3.8 %collective-permute-done.2.right_ref = bf16[2,32,2048]{2,1,0:T(8,128)(2,1)S(1)} collective-permute-done((bf16[2,32,2048]{2,1,0:T(8,128)(2,1)S(1)}, bf16[2,32,2048]{2,1,0:T(8,128)(2,1)S(1)}, u32[]{:S(2)}, u32[]{:S(2)}) %collective-permute-start.2) | collective-permute-done | bytes 262176 | tf_op jit(solution)/shard_map/ppermute | solution.py:294
  19.1 4.1 %collective-permute-done.1.left_ref = bf16[2,32,2048]{2,1,0:T(8,128)(2,1)S(1)} collective-permute-done((bf16[2,32,2048]{2,1,0:T(8,128)(2,1)S(1)}, bf16[2,32,2048]{2,1,0:T(8,128)(2,1)S(1)}, u32[]{:S(2)}, u32[]{:S(2)}) %collective-permute-start.1) | collective-permute-done | bytes 262176 | tf_op jit(solution)/shard_map/ppermute | solution.py:293
  23.2 1.8 %shard_map.101 = bf16[64,16,128]{2,1,0:T(8,128)(2,1)S(1)} custom-call(f32[2]{0:T(128)S(1)} %pad_maximum_fusion.1.scalar_ref, bf16[2,32,2048]{2,1,0:T(8,128)(2,1)S(1)} %shard_map.100.own_ref, bf16[2,32,2048]{2,1,0:T(8,128)(2,1)S(1)} %collective-permute-done.pair_ref, bf16[2,32,2048]{2,1,0:T(8,128)(2,1)S(1)} %collective-permute-done.1.left_ref, ...), custom_call_target="tpu_custom_call" | custom-call | tf_op jit(solution)/shard_map/pallas_call | solution.py:295
  25.0 0.0 copy-start.5
  25.0 0.0 copy-start.9
  25.1 29.9 %all_to_all.5.in_ref = bf16[64,16,128]{2,1,0:T(8,128)(2,1)S(1)} all-to-all(bf16[64,16,128]{2,1,0:T(8,128)(2,1)S(1)} %shard_map.101), channel_id=1, replica_groups=mesh['wa'=64,'gz'=8] {'wa'}, dimensions={0} | all-to-all | bytes 524288 | tf_op jit(solution)/shard_map/all_to_all | solution.py:307
  55.0 0.0 copy-done.9
  55.0 2.4 %shard_map.102 = f32[2,1,32,2048]{3,2,1,0:T(8,128)} custom-call(f32[2]{0:T(128)S(1)} %pad_maximum_fusion.1.scalar_ref, bf16[64,16,128]{2,1,0:T(8,128)(2,1)S(1)} %all_to_all.5.in_ref, bf16[2,256,256]{2,1,0:T(8,128)(2,1)S(1)} %copy-done.5, bf16[2,256,256]{2,1,0:T(8,128)(2,1)S(1)} %copy-done, f32[2,16,128]{2,1,0:T(8,128)S(1)} %copy-done.9, ...), custom_call_target="tpu_custom_call" | custom-call | tf_op jit(solution)/shard_map/pallas_call | solution.py:308
  (9 shorter events, 0.0 us)
Async XLA Ops:
  0.0 1.0 %copy-start.1 = (f32[2,1,32,2048]{3,2,1,0:T(8,128)S(1)}, f32[2,1,32,2048]{3,2,1,0:T(8,128)}, u32[]{:S(2)}) copy-start(f32[2,1,32,2048]{3,2,1,0:T(8,128)} %wave_ref.3) | copy-start | bytes 1572868
  1.0 0.9 %copy-start.4 = (f32[1,32,2048]{2,1,0:T(8,128)S(1)}, f32[1,32,2048]{2,1,0:T(8,128)}, u32[]{:S(2)}) copy-start(f32[1,32,2048]{2,1,0:T(8,128)} %potential_ref.1) | copy-start | bytes 786436
  2.5 3.4 %collective-permute-start = (bf16[2,32,2048]{2,1,0:T(8,128)(2,1)S(1)}, bf16[2,32,2048]{2,1,0:T(8,128)(2,1)S(1)}, u32[]{:S(2)}, u32[]{:S(2)}) collective-permute-start(bf16[2,32,2048]{2,1,0:T(8,128)(2,1)S(1)} %shard_map.100.own_ref), channel_id=1, source_target_pairs={{0,1},{1,0},{2,3},{3,2},{4,5},{5,4},{6,7},{7,6},{8,9},{9,8},{10,11... | collective-permute-start | bytes 786440 | tf_op jit(solution)/shard_map/ppermute | solution.py:287
  6.0 17.2 %copy-start = (bf16[2,256,256]{2,1,0:T(8,128)(2,1)S(1)}, bf16[2,256,256]{2,1,0:T(8,128)(2,1)}, u32[]{:S(2)}) copy-start(bf16[2,256,256]{2,1,0:T(8,128)(2,1)} %constant.61.clone.inv_ref) | copy-start | bytes 786436
  6.0 17.2 %copy-start.2 = (f32[2,16,8,128]{3,2,1,0:T(8,128)S(1)}, f32[2,16,8,128]{3,2,1,0:T(8,128)}, u32[]{:S(2)}) copy-start(f32[2,16,8,128]{3,2,1,0:T(8,128)} %constant.64.clone.rows_ref) | copy-start | bytes 393220
  6.0 17.2 %copy-start.3 = (bf16[2,256,256]{2,1,0:T(8,128)(2,1)S(1)}, bf16[2,256,256]{2,1,0:T(8,128)(2,1)}, u32[]{:S(2)}) copy-start(bf16[2,256,256]{2,1,0:T(8,128)(2,1)} %constant.60.clone.fwd_ref) | copy-start | bytes 786436
  6.0 17.2 %copy-start.7 = (f32[2,16,128]{2,1,0:T(8,128)S(1)}, f32[2,16,128]{2,1,0:T(8,128)}, u32[]{:S(2)}) copy-start(f32[2,16,128]{2,1,0:T(8,128)} %constant.62.clone.tw_ref.tw_i_ref) | copy-start | bytes 49156
  6.2 17.1 %copy-start.6 = (f32[2,16,128]{2,1,0:T(8,128)S(1)}, f32[2,16,128]{2,1,0:T(8,128)}, u32[]{:S(2)}) copy-start(f32[2,16,128]{2,1,0:T(8,128)} %constant.65.clone.step_ref) | copy-start | bytes 49156
  6.2 12.9 %collective-permute-start.2 = (bf16[2,32,2048]{2,1,0:T(8,128)(2,1)S(1)}, bf16[2,32,2048]{2,1,0:T(8,128)(2,1)S(1)}, u32[]{:S(2)}, u32[]{:S(2)}) collective-permute-start(bf16[2,32,2048]{2,1,0:T(8,128)(2,1)S(1)} %get-tuple-element.5), channel_id=1, source_target_pairs={{2,0},{3,1},{4,2},{5,3},{6,4},{7,5},{10,8},{11,9},{12,10},{13,11},... | collective-permute-start | bytes 786440 | tf_op jit(solution)/shard_map/ppermute | solution.py:294
  13.2 10.0 %collective-permute-start.1 = (bf16[2,32,2048]{2,1,0:T(8,128)(2,1)S(1)}, bf16[2,32,2048]{2,1,0:T(8,128)(2,1)S(1)}, u32[]{:S(2)}, u32[]{:S(2)}) collective-permute-start(bf16[2,32,2048]{2,1,0:T(8,128)(2,1)S(1)} %get-tuple-element.6), channel_id=1, source_target_pairs={{0,2},{1,3},{2,4},{3,5},{4,6},{5,7},{8,10},{9,11},{10,12},{11,13},... | collective-permute-start | bytes 786440 | tf_op jit(solution)/shard_map/ppermute | solution.py:293
  15.2 8.1 %copy-start.8 = (f32[16,128]{1,0:T(8,128)S(1)}, f32[16,128]{1,0:T(8,128)}, u32[]{:S(2)}) copy-start(f32[16,128]{1,0:T(8,128)} %constant.63.clone.wave_ref) | copy-start | bytes 24580
  25.0 30.0 %copy-start.5 = (bf16[2,256,256]{2,1,0:T(8,128)(2,1)S(1)}, bf16[2,256,256]{2,1,0:T(8,128)(2,1)}, u32[]{:S(2)}) copy-start(bf16[2,256,256]{2,1,0:T(8,128)(2,1)} %constant.66.clone.fwd_ref) | copy-start | bytes 786436
  25.0 30.0 %copy-start.9 = (f32[2,16,128]{2,1,0:T(8,128)S(1)}, f32[2,16,128]{2,1,0:T(8,128)}, u32[]{:S(2)}) copy-start(f32[2,16,128]{2,1,0:T(8,128)} %constant.67.clone.tw_f_ref) | copy-start | bytes 49156
where the time goes:
time: 57.7 us; the launch traced here: 57.4 us
  blocking collectives  29.9 us (52%)
  starting transfers between devices  10.9 us (19%)
  waiting for transfers between devices  9.41 us (16%)
  Pallas kernels  4.67 us (8%)
  local copies, waits for them, and re-layouts  2.05 us (4%)
    all_to_all x1, blocking collectives, on_device(): chunks = lax.all_to_all(chunks, 'wa', 0, 0, tiled=True)  29.9 us
    ppermute x1, starting transfers between devices, on_device(): right = lax.ppermute(to_left, 'gz', [(i + 2, i) for i in range(6)])  7.07 us
    ppermute x1, waiting for transfers between devices, on_device(): left = lax.ppermute(to_right, 'gz', [(i, i + 2) for i in range(6)])  4.12 us
    ppermute x1, waiting for transfers between devices, on_device(): right = lax.ppermute(to_left, 'gz', [(i + 2, i) for i in range(6)])  3.81 us
    pallas_call x1, Pallas kernels, on_device(): pl.pallas_call(y_kernel, out_shape=jax.ShapeDtypeStruct((2, 1, ROWS, GRID...  2.43 us
    unnamed x20, local copies, waits for them, and re-layouts  2.05 us
    ppermute x1, starting transfers between devices, on_device(): pair = lax.ppermute(own, 'gz', [(i, i ^ 1) for i in range(8)])  1.92 us
    ppermute x1, starting transfers between devices, on_device(): left = lax.ppermute(to_right, 'gz', [(i, i + 2) for i in range(6)])  1.92 us
  transfers between devices with their start and end apart: 3, of which 3 were waited for; matrix products, arithmetic and copies ran while one was open for 0% of the time, Pallas kernels for 0%

commit v1 on v0

--- a/solution.py
+++ b/solution.py
@@ -163,7 +163,7 @@
     )
 
 
-def sweep(load, store, first_row, fwd_ref, inv_ref, tw_f_ref, tw_i_ref, wave_ref, own_ref, step_ref, buf, sign):
+def sweep(load, store, first_row, fwd_ref, inv_ref, tw_f_ref, tw_i_ref, wave_ref, own_ref, step_ref, buf, sign, finish=None):
     for g in range(GROUPS):
         rows = slice(8 * g, 8 * g + 8)
         out = dft16([load(g, c) for c in range(COLS)], 1)
@@ -199,32 +199,56 @@
             terms.append((re, im))
         for c, (re, im) in enumerate(dft16(terms, -1)):
             store(g, c, re, im)
-
-
-def potential_kernel(wave_ref, potential_ref, out_ref):
+        if finish is not None:
+            finish(g)
+
+
+def potential_kernel(wave_hbm, potential_hbm, out_ref, wave_ref, potential_ref, sems):
+    half = GRID // 2
+    blocks = [(slice(16 * g, 16 * g + 16), slice(half * h, half * h + half)) for g in range(2) for h in range(2)]
+    copies = []
+    for b, (rows, at) in enumerate(blocks):
+        copies.append([
+            pltpu.make_async_copy(wave_hbm.at[0, 0, rows, at], wave_ref.at[0, rows, at], sems.at[b, 0]),
+            pltpu.make_async_copy(wave_hbm.at[1, 0, rows, at], wave_ref.at[1, rows, at], sems.at[b, 1]),
+            pltpu.make_async_copy(potential_hbm.at[0, rows, at], potential_ref.at[rows, at], sems.at[b, 2]),
+        ])
+        for copy in copies[-1]:
+            copy.start()
+    for (rows, at), waits in zip(blocks, copies):
+        for copy in waits:
+            copy.wait()
+        for first in range(at.start, at.stop, LANES):
+            cols = slice(first, first + LANES)
+            re, im, pot = wave_ref[0, rows, cols], wave_ref[1, rows, cols], potential_ref[rows, cols]
+            sine, cosine = sincos(time_step * (pot + coupling * (re * re + im * im)))
+            out_ref[0, rows, cols] = (re * cosine + im * sine).astype(jnp.bfloat16)
+            out_ref[1, rows, cols] = (im * cosine - re * sine).astype(jnp.bfloat16)
+
+
+def message_kernel(own_ref, pair_ref, out_ref):
     for g in range(2):
         rows = slice(16 * g, 16 * g + 16)
         for c in range(COLS):
             at = slice(LANES * c, LANES * c + LANES)
-            re, im, pot = wave_ref[0, 0, rows, at], wave_ref[1, 0, rows, at], potential_ref[0, rows, at]
-            sine, cosine = sincos(time_step * (pot + coupling * (re * re + im * im)))
-            out_ref[0, rows, at] = (re * cosine + im * sine).astype(jnp.bfloat16)
-            out_ref[1, rows, at] = (im * cosine - re * sine).astype(jnp.bfloat16)
-
-
-def x_kernel(scalar_ref, own_ref, pair_ref, left_ref, right_ref, fwd_ref, inv_ref, tw_ref, wave_ref, rows_ref, step_ref, out_ref, mixed, buf, swept):
+            re, im, pre, pim = (ref[p, rows, at].astype(jnp.float32) for ref in (own_ref, pair_ref) for p in range(2))
+            out_ref[0, rows, at] = (FAR * re + NEAR[0] * pre - NEAR[1] * pim).astype(jnp.bfloat16)
+            out_ref[1, rows, at] = (FAR * im + NEAR[0] * pim + NEAR[1] * pre).astype(jnp.bfloat16)
+
+
+def x_kernel(scalar_ref, own_ref, pair_ref, far_ref, sum_ref, fwd_ref, inv_ref, tw_ref, wave_ref, rows_ref, step_ref, out_ref, mixed, buf, swept):
     centre = scalar_ref[1]
     for g in range(2):
         rows = slice(16 * g, 16 * g + 16)
         for c in range(COLS):
             at = slice(LANES * c, LANES * c + LANES)
-            re, im, pre, pim, lre, lim, rre, rim = (
+            re, im, pre, pim, fre, fim, sre, sim = (
                 ref[p, rows, at].astype(jnp.float32)
-                for ref in (own_ref, pair_ref, left_ref, right_ref)
+                for ref in (own_ref, pair_ref, far_ref, sum_ref)
                 for p in range(2)
             )
-            mixed[0, rows, at] = centre * re - CENTRE[1] * im + (NEAR[0] * pre - NEAR[1] * pim) + (lre + rre)
-            mixed[1, rows, at] = centre * im + CENTRE[1] * re + (NEAR[0] * pim + NEAR[1] * pre) + (lim + rim)
+            mixed[0, rows, at] = centre * re - CENTRE[1] * im + (NEAR[0] * pre - NEAR[1] * pim) + (FAR * fre + sre)
+            mixed[1, rows, at] = centre * im + CENTRE[1] * re + (NEAR[0] * pim + NEAR[1] * pre) + (FAR * fim + sim)
 
     def load(g, c):
         at = slice(LANES * c, LANES * c + LANES)
@@ -242,7 +266,7 @@
             out_ref[4 * c + q] = jnp.concatenate([re[q], im[q]], axis=0).astype(jnp.bfloat16)
 
 
-def y_kernel(scalar_ref, in_ref, fwd_ref, inv_ref, tw_f_ref, tw_i_ref, wave_ref, rows_ref, step_ref, out_ref, field, buf):
+def y_kernel(scalar_ref, in_ref, fwd_ref, inv_ref, tw_f_ref, tw_i_ref, wave_ref, rows_ref, step_ref, out_hbm, field, buf, out_ref, sems):
     for s in range(4):
         block = in_ref[16 * s : 16 * s + 16].astype(jnp.float32)
         for p in range(2):
@@ -258,13 +282,24 @@
 
     def store(g, c, re, im):
         at = slice(LANES * c, LANES * c + LANES)
-        out_ref[0, 0, 8 * g : 8 * g + 8, at] = re
-        out_ref[1, 0, 8 * g : 8 * g + 8, at] = im
-
-    sweep(load, store, scalar_ref[0], fwd_ref, inv_ref, tw_f_ref, tw_i_ref, wave_ref, rows_ref, step_ref, buf, -1.0)
+        out_ref[0, 8 * g : 8 * g + 8, at] = re
+        out_ref[1, 8 * g : 8 * g + 8, at] = im
+
+    copies = []
+
+    def send(g):
+        rows = slice(8 * g, 8 * g + 8)
+        for p in range(2):
+            copies.append(pltpu.make_async_copy(out_ref.at[p, rows], out_hbm.at[p, 0, rows], sems.at[g, p]))
+            copies[-1].start()
+
+    sweep(load, store, scalar_ref[0], fwd_ref, inv_ref, tw_f_ref, tw_i_ref, wave_ref, rows_ref, step_ref, buf, -1.0, send)
+    for copy in copies:
+        copy.wait()
 
 
 SMEM = pl.BlockSpec(memory_space=pltpu.SMEM)
+HBM = pl.BlockSpec(memory_space=pltpu.HBM)
 VMEM = pl.BlockSpec(memory_space=pltpu.VMEM)
 PARAMS = pltpu.CompilerParams(vmem_limit_bytes=48 * 1024 * 1024)
 
@@ -275,23 +310,29 @@
     row_base = lax.axis_index("wa") * ROWS - GRID // 2
     plane = lax.axis_index("gz")
     edge = (plane == 0) | (plane == 7)
-    odd = (plane % 2).astype(f32)
     scalars = jnp.stack([row_base.astype(f32) * spacing, jnp.where(edge, CENTRE_EDGE, CENTRE[0])])
     own = pl.pallas_call(
         potential_kernel,
         out_shape=jax.ShapeDtypeStruct((2, ROWS, GRID), bf16),
+        in_specs=[HBM, HBM],
+        out_specs=VMEM,
+        scratch_shapes=[
+            pltpu.VMEM((2, ROWS, GRID), f32),
+            pltpu.VMEM((ROWS, GRID), f32),
+            pltpu.SemaphoreType.DMA((4, 3)),
+        ],
+        compiler_params=PARAMS,
+    )(pltpu.with_memory_space_constraint(wave, pltpu.HBM), pltpu.with_memory_space_constraint(potential, pltpu.HBM))
+    far = lax.ppermute(own, "gz", [(i, i - 2) for i in (2, 4, 6)] + [(i, i + 2) for i in (1, 3, 5)])
+    pair = lax.ppermute(own, "gz", [(i, i ^ 1) for i in range(8)])
+    message = pl.pallas_call(
+        message_kernel,
+        out_shape=jax.ShapeDtypeStruct((2, ROWS, GRID), bf16),
         in_specs=[VMEM, VMEM],
         out_specs=VMEM,
         compiler_params=PARAMS,
-    )(wave, potential)
-    pair = lax.ppermute(own, "gz", [(i, i ^ 1) for i in range(8)])
-    far = FAR * own.astype(f32)
-    pr, pi = pair[0].astype(f32), pair[1].astype(f32)
-    near = jnp.stack([NEAR[0] * pr - NEAR[1] * pi, NEAR[0] * pi + NEAR[1] * pr])
-    to_right = (far + (1.0 - odd) * near).astype(bf16)
-    to_left = (far + odd * near).astype(bf16)
-    left = lax.ppermute(to_right, "gz", [(i, i + 2) for i in range(6)])
-    right = lax.ppermute(to_left, "gz", [(i + 2, i) for i in range(6)])
+    )(own, pair)
+    summed = lax.ppermute(message, "gz", [(i, i + 2) for i in (0, 2, 4)] + [(i, i - 2) for i in (3, 5, 7)])
     chunks = pl.pallas_call(
         x_kernel,
         out_shape=jax.ShapeDtypeStruct((PARTS_WA, 16, LANES), bf16),
@@ -303,16 +344,18 @@
             pltpu.VMEM((COLS, 2, GROUPS, 8, LANES), f32),
         ],
         compiler_params=PARAMS,
-    )(scalars, own, pair, left, right, t["fwd_x"], t["inv"], t["tw_x"], t["wavenum"], t["own"], t["step8"])
+    )(scalars, own, pair, far, summed, t["fwd_x"], t["inv"], t["tw_x"], t["wavenum"], t["own"], t["step8"])
     chunks = lax.all_to_all(chunks, "wa", 0, 0, tiled=True)
     return pl.pallas_call(
         y_kernel,
         out_shape=jax.ShapeDtypeStruct((2, 1, ROWS, GRID), f32),
         in_specs=[SMEM] + [VMEM] * 8,
-        out_specs=VMEM,
+        out_specs=HBM,
         scratch_shapes=[
             pltpu.VMEM((2, ROWS, GRID), f32),
             pltpu.VMEM((COLS, ROWS, 2 * LANES), f32),
+            pltpu.VMEM((2, ROWS, GRID), f32),
+            pltpu.SemaphoreType.DMA((GROUPS, 2)),
         ],
         compiler_params=PARAMS,
     )(scalars, chunks, t["fwd_y"], t["inv"], t["tw_y"], t["tw_x"], t["wavenum"], t["own"], t["step8"])

time: 57.7 us -> 55 us (0.953)
  the two profiles are of different devices: /device:TPU:64 before, /device:TPU:1 now
where the time goes in v1:
time: 55 us; the launch traced here: 54.7 us
  blocking collectives  29.5 us (54%)
  starting transfers between devices  11.5 us (21%)
  waiting for transfers between devices  7.5 us (14%)
  Pallas kernels  5.91 us (11%)
    all_to_all x1, blocking collectives, on_device(): chunks = lax.all_to_all(chunks, 'wa', 0, 0, tiled=True)  29.5 us
    ppermute x1, starting transfers between devices, on_device(): pair = lax.ppermute(own, 'gz', [(i, i ^ 1) for i in range(8)])  8.92 us
    ppermute x1, waiting for transfers between devices, on_device(): lax.ppermute(message, 'gz', [(i, i + 2) for i in (0, 2, 4)] + [(i, i - 2)...  5.8 us
    pallas_call x1, Pallas kernels, on_device(): pl.pallas_call(y_kernel, out_shape=jax.ShapeDtypeStruct((2, 1, ROWS, GRID...  2.44 us
    pallas_call x1, Pallas kernels, on_device(): pl.pallas_call(x_kernel, out_shape=jax.ShapeDtypeStruct((PARTS_WA, 16, LA...  1.79 us
    ppermute x1, waiting for transfers between devices, on_device(): lax.ppermute(own, 'gz', [(i, i - 2) for i in (2, 4, 6)] + [(i, i + 2) for...  1.7 us
    pallas_call x1, Pallas kernels, on_device(): pl.pallas_call(potential_kernel, out_shape=jax.ShapeDtypeStruct((2, ROWS,...  1.54 us
    ppermute x1, starting transfers between devices, on_device(): lax.ppermute(own, 'gz', [(i, i - 2) for i in (2, 4, 6)] + [(i, i + 2) for...  1.31 us
  transfers between devices with their start and end apart: 3, of which 2 were waited for; matrix products, arithmetic and copies ran while one was open for 0% of the time, Pallas kernels for 0%

profile of v1, /device:TPU:1, one launch (start us, length us, event | category | flops | bytes accessed | tf_op | source)
XLA Modules:
  0.0 54.7 jit_solution(17237408503030166053)
XLA Ops:
  0.0 1.5 %shard_map.100.own_ref = bf16[2,32,2048]{2,1,0:T(8,128)(2,1)S(1)} custom-call(f32[2,1,32,2048]{3,2,1,0:T(8,128)} %wave_hbm.1, f32[1,32,2048]{2,1,0:T(8,128)} %potential_hbm.1), custom_call_target="tpu_custom_call" | custom-call | tf_op jit(solution)/shard_map/pallas_call | solution.py:314
  1.5 0.0 copy-start
  1.6 0.0 copy-start.1
  1.6 0.0 copy-start.2
  1.6 8.9 %collective-permute-start = (bf16[2,32,2048]{2,1,0:T(8,128)(2,1)S(1)}, bf16[2,32,2048]{2,1,0:T(8,128)(2,1)S(1)}, u32[]{:S(2)}, u32[]{:S(2)}) collective-permute-start(bf16[2,32,2048]{2,1,0:T(8,128)(2,1)S(1)} %shard_map.100.own_ref), channel_id=1, source_target_pairs={{0,1},{1,0},{2,3},{3,2},{4,5},{5,4},{6,7},{7,6},{8,9},{9,8},{10,11... | collective-permute-start | bytes 786440 | tf_op jit(solution)/shard_map/ppermute | solution.py:327
  10.5 1.3 %collective-permute-start.1 = (bf16[2,32,2048]{2,1,0:T(8,128)(2,1)S(1)}, bf16[2,32,2048]{2,1,0:T(8,128)(2,1)S(1)}, u32[]{:S(2)}, u32[]{:S(2)}) collective-permute-start(bf16[2,32,2048]{2,1,0:T(8,128)(2,1)S(1)} %shard_map.100.own_ref), channel_id=1, source_target_pairs={{2,0},{4,2},{6,4},{1,3},{3,5},{5,7},{10,8},{12,10},{14,12},{9,11},... | collective-permute-start | bytes 786440 | tf_op jit(solution)/shard_map/ppermute | solution.py:326
  11.8 0.0 collective-permute-done.pair_ref
  11.8 0.0 copy-start.6
  11.8 0.1 shard_map.101
  12.0 0.0 copy-start.4
  12.0 0.0 copy-start.5
  12.0 1.3 %collective-permute-start.2 = (bf16[2,32,2048]{2,1,0:T(8,128)(2,1)S(1)}, bf16[2,32,2048]{2,1,0:T(8,128)(2,1)S(1)}, u32[]{:S(2)}, u32[]{:S(2)}) collective-permute-start(bf16[2,32,2048]{2,1,0:T(8,128)(2,1)S(1)} %shard_map.101), channel_id=1, source_target_pairs={{0,2},{2,4},{4,6},{3,1},{5,3},{7,5},{8,10},{10,12},{12,14},{11,9},... | collective-permute-start | bytes 786440 | tf_op jit(solution)/shard_map/ppermute | solution.py:335
  13.3 0.1 pad_maximum_fusion.scalar_ref
  13.4 1.7 %collective-permute-done.1.far_ref = bf16[2,32,2048]{2,1,0:T(8,128)(2,1)S(1)} collective-permute-done((bf16[2,32,2048]{2,1,0:T(8,128)(2,1)S(1)}, bf16[2,32,2048]{2,1,0:T(8,128)(2,1)S(1)}, u32[]{:S(2)}, u32[]{:S(2)}) %collective-permute-start.1) | collective-permute-done | bytes 262176 | tf_op jit(solution)/shard_map/ppermute | solution.py:326
  15.1 5.8 %collective-permute-done.2.sum_ref = bf16[2,32,2048]{2,1,0:T(8,128)(2,1)S(1)} collective-permute-done((bf16[2,32,2048]{2,1,0:T(8,128)(2,1)S(1)}, bf16[2,32,2048]{2,1,0:T(8,128)(2,1)S(1)}, u32[]{:S(2)}, u32[]{:S(2)}) %collective-permute-start.2) | collective-permute-done | bytes 262176 | tf_op jit(solution)/shard_map/ppermute | solution.py:335
  20.9 0.0 copy-done
  20.9 0.0 copy-done.1
  20.9 0.0 copy-done.2
  20.9 1.8 %shard_map.102 = bf16[64,16,128]{2,1,0:T(8,128)(2,1)S(1)} custom-call(f32[2]{0:T(128)S(1)} %pad_maximum_fusion.scalar_ref, bf16[2,32,2048]{2,1,0:T(8,128)(2,1)S(1)} %shard_map.100.own_ref, bf16[2,32,2048]{2,1,0:T(8,128)(2,1)S(1)} %collective-permute-done.pair_ref, bf16[2,32,2048]{2,1,0:T(8,128)(2,1)S(1)} %collective-permute-done.1.far_ref, ...), custom_call_target="tpu_custom_call" | custom-call | tf_op jit(solution)/shard_map/pallas_call | solution.py:336
  22.7 0.0 copy-start.3
  22.8 0.0 copy-start.7
  22.8 29.5 %all_to_all.5.in_ref = bf16[64,16,128]{2,1,0:T(8,128)(2,1)S(1)} all-to-all(bf16[64,16,128]{2,1,0:T(8,128)(2,1)S(1)} %shard_map.102), channel_id=1, replica_groups=mesh['wa'=64,'gz'=8] {'wa'}, dimensions={0} | all-to-all | bytes 524288 | tf_op jit(solution)/shard_map/all_to_all | solution.py:348
  52.3 0.0 copy-done.7
  52.3 2.4 %shard_map.103 = f32[2,1,32,2048]{3,2,1,0:T(8,128)} custom-call(f32[2]{0:T(128)S(1)} %pad_maximum_fusion.scalar_ref, bf16[64,16,128]{2,1,0:T(8,128)(2,1)S(1)} %all_to_all.5.in_ref, bf16[2,256,256]{2,1,0:T(8,128)(2,1)S(1)} %copy-done.3, bf16[2,256,256]{2,1,0:T(8,128)(2,1)S(1)} %copy-done, f32[2,16,128]{2,1,0:T(8,128)S(1)} %copy-done.7, ...), custom_call_target="tpu_custom_call" | custom-call | tf_op jit(solution)/shard_map/pallas_call | solution.py:349
  (4 shorter events, 0.0 us)
Async XLA Ops:
  1.5 19.4 %copy-start = (bf16[2,256,256]{2,1,0:T(8,128)(2,1)S(1)}, bf16[2,256,256]{2,1,0:T(8,128)(2,1)}, u32[]{:S(2)}) copy-start(bf16[2,256,256]{2,1,0:T(8,128)(2,1)} %constant.41.clone.inv_ref) | copy-start | bytes 786436
  1.6 19.4 %copy-start.1 = (f32[2,16,8,128]{3,2,1,0:T(8,128)S(1)}, f32[2,16,8,128]{3,2,1,0:T(8,128)}, u32[]{:S(2)}) copy-start(f32[2,16,8,128]{3,2,1,0:T(8,128)} %constant.44.clone.rows_ref) | copy-start | bytes 393220
  1.6 19.3 %copy-start.2 = (bf16[2,256,256]{2,1,0:T(8,128)(2,1)S(1)}, bf16[2,256,256]{2,1,0:T(8,128)(2,1)}, u32[]{:S(2)}) copy-start(bf16[2,256,256]{2,1,0:T(8,128)(2,1)} %constant.40.clone.fwd_ref) | copy-start | bytes 786436
  1.6 10.2 %collective-permute-start = (bf16[2,32,2048]{2,1,0:T(8,128)(2,1)S(1)}, bf16[2,32,2048]{2,1,0:T(8,128)(2,1)S(1)}, u32[]{:S(2)}, u32[]{:S(2)}) collective-permute-start(bf16[2,32,2048]{2,1,0:T(8,128)(2,1)S(1)} %shard_map.100.own_ref), channel_id=1, source_target_pairs={{0,1},{1,0},{2,3},{3,2},{4,5},{5,4},{6,7},{7,6},{8,9},{9,8},{10,11... | collective-permute-start | bytes 786440 | tf_op jit(solution)/shard_map/ppermute | solution.py:327
  10.5 4.6 %collective-permute-start.1 = (bf16[2,32,2048]{2,1,0:T(8,128)(2,1)S(1)}, bf16[2,32,2048]{2,1,0:T(8,128)(2,1)S(1)}, u32[]{:S(2)}, u32[]{:S(2)}) collective-permute-start(bf16[2,32,2048]{2,1,0:T(8,128)(2,1)S(1)} %shard_map.100.own_ref), channel_id=1, source_target_pairs={{2,0},{4,2},{6,4},{1,3},{3,5},{5,7},{10,8},{12,10},{14,12},{9,11},... | collective-permute-start | bytes 786440 | tf_op jit(solution)/shard_map/ppermute | solution.py:326
  11.8 9.1 %copy-start.6 = (f32[16,128]{1,0:T(8,128)S(1)}, f32[16,128]{1,0:T(8,128)}, u32[]{:S(2)}) copy-start(f32[16,128]{1,0:T(8,128)} %constant.43.clone.wave_ref) | copy-start | bytes 24580
  12.0 8.9 %copy-start.4 = (f32[2,16,128]{2,1,0:T(8,128)S(1)}, f32[2,16,128]{2,1,0:T(8,128)}, u32[]{:S(2)}) copy-start(f32[2,16,128]{2,1,0:T(8,128)} %constant.42.clone.tw_ref.tw_i_ref) | copy-start | bytes 49156
  12.0 8.9 %copy-start.5 = (f32[2,16,128]{2,1,0:T(8,128)S(1)}, f32[2,16,128]{2,1,0:T(8,128)}, u32[]{:S(2)}) copy-start(f32[2,16,128]{2,1,0:T(8,128)} %constant.45.clone.step_ref) | copy-start | bytes 49156
  12.0 8.9 %collective-permute-start.2 = (bf16[2,32,2048]{2,1,0:T(8,128)(2,1)S(1)}, bf16[2,32,2048]{2,1,0:T(8,128)(2,1)S(1)}, u32[]{:S(2)}, u32[]{:S(2)}) collective-permute-start(bf16[2,32,2048]{2,1,0:T(8,128)(2,1)S(1)} %shard_map.101), channel_id=1, source_target_pairs={{0,2},{2,4},{4,6},{3,1},{5,3},{7,5},{8,10},{10,12},{12,14},{11,9},... | collective-permute-start | bytes 786440 | tf_op jit(solution)/shard_map/ppermute | solution.py:335
  22.7 29.5 %copy-start.3 = (bf16[2,256,256]{2,1,0:T(8,128)(2,1)S(1)}, bf16[2,256,256]{2,1,0:T(8,128)(2,1)}, u32[]{:S(2)}) copy-start(bf16[2,256,256]{2,1,0:T(8,128)(2,1)} %constant.46.clone.fwd_ref) | copy-start | bytes 786436
  22.8 29.5 %copy-start.7 = (f32[2,16,128]{2,1,0:T(8,128)S(1)}, f32[2,16,128]{2,1,0:T(8,128)}, u32[]{:S(2)}) copy-start(f32[2,16,128]{2,1,0:T(8,128)} %constant.47.clone.tw_f_ref) | copy-start | bytes 49156

commit v2 on v1

--- a/solution.py
+++ b/solution.py
@@ -226,29 +226,25 @@
             out_ref[1, rows, cols] = (im * cosine - re * sine).astype(jnp.bfloat16)
 
 
-def message_kernel(own_ref, pair_ref, out_ref):
-    for g in range(2):
-        rows = slice(16 * g, 16 * g + 16)
-        for c in range(COLS):
-            at = slice(LANES * c, LANES * c + LANES)
-            re, im, pre, pim = (ref[p, rows, at].astype(jnp.float32) for ref in (own_ref, pair_ref) for p in range(2))
-            out_ref[0, rows, at] = (FAR * re + NEAR[0] * pre - NEAR[1] * pim).astype(jnp.bfloat16)
-            out_ref[1, rows, at] = (FAR * im + NEAR[0] * pim + NEAR[1] * pre).astype(jnp.bfloat16)
-
-
-def x_kernel(scalar_ref, own_ref, pair_ref, far_ref, sum_ref, fwd_ref, inv_ref, tw_ref, wave_ref, rows_ref, step_ref, out_ref, mixed, buf, swept):
+def message_kernel(own_ref, far_ref, out_ref):
+    for p in range(2):
+        total = own_ref[p].astype(jnp.float32) + far_ref[p].astype(jnp.float32)
+        out_ref[p] = total.astype(jnp.bfloat16)
+
+
+def x_kernel(scalar_ref, own_ref, near_ref, far_ref, across_ref, fwd_ref, inv_ref, tw_ref, wave_ref, rows_ref, step_ref, out_ref, mixed, buf, swept):
     centre = scalar_ref[1]
     for g in range(2):
         rows = slice(16 * g, 16 * g + 16)
         for c in range(COLS):
             at = slice(LANES * c, LANES * c + LANES)
-            re, im, pre, pim, fre, fim, sre, sim = (
+            re, im, nre, nim, fre, fim, are, aim = (
                 ref[p, rows, at].astype(jnp.float32)
-                for ref in (own_ref, pair_ref, far_ref, sum_ref)
+                for ref in (own_ref, near_ref, far_ref, across_ref)
                 for p in range(2)
             )
-            mixed[0, rows, at] = centre * re - CENTRE[1] * im + (NEAR[0] * pre - NEAR[1] * pim) + (FAR * fre + sre)
-            mixed[1, rows, at] = centre * im + CENTRE[1] * re + (NEAR[0] * pim + NEAR[1] * pre) + (FAR * fim + sim)
+            mixed[0, rows, at] = centre * re - CENTRE[1] * im + (NEAR[0] * nre - NEAR[1] * nim) + FAR * (fre + are)
+            mixed[1, rows, at] = centre * im + CENTRE[1] * re + (NEAR[0] * nim + NEAR[1] * nre) + FAR * (fim + aim)
 
     def load(g, c):
         at = slice(LANES * c, LANES * c + LANES)
@@ -323,16 +319,18 @@
         ],
         compiler_params=PARAMS,
     )(pltpu.with_memory_space_constraint(wave, pltpu.HBM), pltpu.with_memory_space_constraint(potential, pltpu.HBM))
-    far = lax.ppermute(own, "gz", [(i, i - 2) for i in (2, 4, 6)] + [(i, i + 2) for i in (1, 3, 5)])
-    pair = lax.ppermute(own, "gz", [(i, i ^ 1) for i in range(8)])
+    outward = [(i, i - 2) for i in (2, 4, 6)] + [(i, i + 2) for i in (1, 3, 5)]
+    inward = [(i, i + 2) for i in (0, 2, 4)] + [(i, i - 2) for i in (3, 5, 7)]
+    far = lax.ppermute(own, "gz", outward)
+    across = lax.ppermute(own, "gz", inward)
     message = pl.pallas_call(
         message_kernel,
         out_shape=jax.ShapeDtypeStruct((2, ROWS, GRID), bf16),
         in_specs=[VMEM, VMEM],
         out_specs=VMEM,
         compiler_params=PARAMS,
-    )(own, pair)
-    summed = lax.ppermute(message, "gz", [(i, i + 2) for i in (0, 2, 4)] + [(i, i - 2) for i in (3, 5, 7)])
+    )(own, far)
+    near = lax.ppermute(message, "gz", [(i, i ^ 1) for i in range(8)])
     chunks = pl.pallas_call(
         x_kernel,
         out_shape=jax.ShapeDtypeStruct((PARTS_WA, 16, LANES), bf16),
@@ -344,7 +342,7 @@
             pltpu.VMEM((COLS, 2, GROUPS, 8, LANES), f32),
         ],
         compiler_params=PARAMS,
-    )(scalars, own, pair, far, summed, t["fwd_x"], t["inv"], t["tw_x"], t["wavenum"], t["own"], t["step8"])
+    )(scalars, own, near, far, across, t["fwd_x"], t["inv"], t["tw_x"], t["wavenum"], t["own"], t["step8"])
     chunks = lax.all_to_all(chunks, "wa", 0, 0, tiled=True)
     return pl.pallas_call(
         y_kernel,

time: 55 us -> 54.3 us (0.987); the launches traced: 54.7 us -> 53.4 us
  starting transfers between devices: 11.5 us -> 16.1 us
  waiting for transfers between devices: 7.5 us -> 3.03 us
  blocking collectives: 29.5 us -> 28.1 us
    ppermute x3, starting transfers between devices: 11.5 us -> 16.1 us  [the longest x1 9.87 us: on_device(): near = lax.ppermute(message, 'gz', [(i, i ^ 1) for i in range(8)])]
    ppermute x3, waiting for transfers between devices: 7.5 us -> 3.03 us  [the longest x1 1.98 us: on_device(): far = lax.ppermute(own, 'gz', outward)]
    all_to_all x1, blocking collectives: 29.5 us -> 28.1 us  [on_device(): chunks = lax.all_to_all(chunks, 'wa', 0, 0, tiled=True)]
where the time goes in v2:
time: 54.3 us; the launch traced here: 53.4 us
  blocking collectives  28.1 us (52%)
  starting transfers between devices  16.1 us (30%)
  Pallas kernels  5.83 us (11%)
  waiting for transfers between devices  3.03 us (6%)
    all_to_all x1, blocking collectives, on_device(): chunks = lax.all_to_all(chunks, 'wa', 0, 0, tiled=True)  28.1 us
    ppermute x1, starting transfers between devices, on_device(): near = lax.ppermute(message, 'gz', [(i, i ^ 1) for i in range(8)])  9.87 us
    ppermute x1, starting transfers between devices, on_device(): far = lax.ppermute(own, 'gz', outward)  4.97 us
    pallas_call x1, Pallas kernels, on_device(): pl.pallas_call(y_kernel, out_shape=jax.ShapeDtypeStruct((2, 1, ROWS, GRID...  2.44 us
    ppermute x1, waiting for transfers between devices, on_device(): far = lax.ppermute(own, 'gz', outward)  1.98 us
    pallas_call x1, Pallas kernels, on_device(): pl.pallas_call(x_kernel, out_shape=jax.ShapeDtypeStruct((PARTS_WA, 16, LA...  1.79 us
    pallas_call x1, Pallas kernels, on_device(): pl.pallas_call(potential_kernel, out_shape=jax.ShapeDtypeStruct((2, ROWS,...  1.54 us
    ppermute x1, starting transfers between devices, on_device(): across = lax.ppermute(own, 'gz', inward)  1.29 us
  transfers between devices with their start and end apart: 3, of which 2 were waited for; matrix products, arithmetic and copies ran while one was open for 0% of the time, Pallas kernels for 0%

profile of v2, /device:TPU:1, one launch (start us, length us, event | category | flops | bytes accessed | tf_op | source)
XLA Modules:
  0.0 53.4 jit_solution(6591874350392669376)
XLA Ops:
  0.0 1.5 %shard_map.100.own_ref = bf16[2,32,2048]{2,1,0:T(8,128)(2,1)S(1)} custom-call(f32[2,1,32,2048]{3,2,1,0:T(8,128)} %wave_hbm.1, f32[1,32,2048]{2,1,0:T(8,128)} %potential_hbm.1), custom_call_target="tpu_custom_call" | custom-call | tf_op jit(solution)/shard_map/pallas_call | solution.py:310
  1.5 0.0 copy-start
  1.6 0.0 copy-start.1
  1.6 0.0 copy-start.2
  1.6 5.0 %collective-permute-start = (bf16[2,32,2048]{2,1,0:T(8,128)(2,1)S(1)}, bf16[2,32,2048]{2,1,0:T(8,128)(2,1)S(1)}, u32[]{:S(2)}, u32[]{:S(2)}) collective-permute-start(bf16[2,32,2048]{2,1,0:T(8,128)(2,1)S(1)} %shard_map.100.own_ref), channel_id=1, source_target_pairs={{2,0},{4,2},{6,4},{1,3},{3,5},{5,7},{10,8},{12,10},{14,12},{9,11},... | collective-permute-start | bytes 786440 | tf_op jit(solution)/shard_map/ppermute | solution.py:324
  6.6 1.3 %collective-permute-start.2 = (bf16[2,32,2048]{2,1,0:T(8,128)(2,1)S(1)}, bf16[2,32,2048]{2,1,0:T(8,128)(2,1)S(1)}, u32[]{:S(2)}, u32[]{:S(2)}) collective-permute-start(bf16[2,32,2048]{2,1,0:T(8,128)(2,1)S(1)} %shard_map.100.own_ref), channel_id=1, source_target_pairs={{0,2},{2,4},{4,6},{3,1},{5,3},{7,5},{8,10},{10,12},{12,14},{11,9},... | collective-permute-start | bytes 786440 | tf_op jit(solution)/shard_map/ppermute | solution.py:325
  7.9 2.0 %collective-permute-done.far_ref = bf16[2,32,2048]{2,1,0:T(8,128)(2,1)S(1)} collective-permute-done((bf16[2,32,2048]{2,1,0:T(8,128)(2,1)S(1)}, bf16[2,32,2048]{2,1,0:T(8,128)(2,1)S(1)}, u32[]{:S(2)}, u32[]{:S(2)}) %collective-permute-start) | collective-permute-done | bytes 262176 | tf_op jit(solution)/shard_map/ppermute | solution.py:324
  9.8 0.1 shard_map.101
  9.9 0.0 copy-start.4
  9.9 0.0 copy-start.5
  9.9 9.9 %collective-permute-start.1 = (bf16[2,32,2048]{2,1,0:T(8,128)(2,1)S(1)}, bf16[2,32,2048]{2,1,0:T(8,128)(2,1)S(1)}, u32[]{:S(2)}, u32[]{:S(2)}) collective-permute-start(bf16[2,32,2048]{2,1,0:T(8,128)(2,1)S(1)} %shard_map.101), channel_id=1, source_target_pairs={{0,1},{1,0},{2,3},{3,2},{4,5},{5,4},{6,7},{7,6},{8,9},{9,8},{10,11... | collective-permute-start | bytes 786440 | tf_op jit(solution)/shard_map/ppermute | solution.py:333
  19.8 0.1 pad_maximum_fusion.scalar_ref
  19.9 0.0 collective-permute-done.2.across_ref
  19.9 1.0 %collective-permute-done.1.near_ref = bf16[2,32,2048]{2,1,0:T(8,128)(2,1)S(1)} collective-permute-done((bf16[2,32,2048]{2,1,0:T(8,128)(2,1)S(1)}, bf16[2,32,2048]{2,1,0:T(8,128)(2,1)S(1)}, u32[]{:S(2)}, u32[]{:S(2)}) %collective-permute-start.1) | collective-permute-done | bytes 262176 | tf_op jit(solution)/shard_map/ppermute | solution.py:333
  21.0 0.0 copy-done
  21.0 0.0 copy-done.1
  21.0 0.0 copy-done.2
  21.0 0.0 copy-done.6
  21.0 1.8 %shard_map.102 = bf16[64,16,128]{2,1,0:T(8,128)(2,1)S(1)} custom-call(f32[2]{0:T(128)S(1)} %pad_maximum_fusion.scalar_ref, bf16[2,32,2048]{2,1,0:T(8,128)(2,1)S(1)} %shard_map.100.own_ref, bf16[2,32,2048]{2,1,0:T(8,128)(2,1)S(1)} %collective-permute-done.1.near_ref, bf16[2,32,2048]{2,1,0:T(8,128)(2,1)S(1)} %collective-permute-done.far_ref, ...), custom_call_target="tpu_custom_call" | custom-call | tf_op jit(solution)/shard_map/pallas_call | solution.py:334
  22.8 0.0 copy-start.3
  22.8 0.0 copy-start.7
  22.8 28.1 %all_to_all.5.in_ref = bf16[64,16,128]{2,1,0:T(8,128)(2,1)S(1)} all-to-all(bf16[64,16,128]{2,1,0:T(8,128)(2,1)S(1)} %shard_map.102), channel_id=1, replica_groups=mesh['wa'=64,'gz'=8] {'wa'}, dimensions={0} | all-to-all | bytes 524288 | tf_op jit(solution)/shard_map/all_to_all | solution.py:346
  50.9 0.0 copy-done.7
  50.9 2.4 %shard_map.103 = f32[2,1,32,2048]{3,2,1,0:T(8,128)} custom-call(f32[2]{0:T(128)S(1)} %pad_maximum_fusion.scalar_ref, bf16[64,16,128]{2,1,0:T(8,128)(2,1)S(1)} %all_to_all.5.in_ref, bf16[2,256,256]{2,1,0:T(8,128)(2,1)S(1)} %copy-done.3, bf16[2,256,256]{2,1,0:T(8,128)(2,1)S(1)} %copy-done, f32[2,16,128]{2,1,0:T(8,128)S(1)} %copy-done.7, ...), custom_call_target="tpu_custom_call" | custom-call | tf_op jit(solution)/shard_map/pallas_call | solution.py:347
  (4 shorter events, 0.0 us)
Async XLA Ops:
  1.5 19.4 %copy-start = (bf16[2,256,256]{2,1,0:T(8,128)(2,1)S(1)}, bf16[2,256,256]{2,1,0:T(8,128)(2,1)}, u32[]{:S(2)}) copy-start(bf16[2,256,256]{2,1,0:T(8,128)(2,1)} %constant.41.clone.inv_ref) | copy-start | bytes 786436
  1.6 19.4 %copy-start.1 = (f32[2,16,8,128]{3,2,1,0:T(8,128)S(1)}, f32[2,16,8,128]{3,2,1,0:T(8,128)}, u32[]{:S(2)}) copy-start(f32[2,16,8,128]{3,2,1,0:T(8,128)} %constant.44.clone.rows_ref) | copy-start | bytes 393220
  1.6 19.4 %copy-start.2 = (bf16[2,256,256]{2,1,0:T(8,128)(2,1)S(1)}, bf16[2,256,256]{2,1,0:T(8,128)(2,1)}, u32[]{:S(2)}) copy-start(bf16[2,256,256]{2,1,0:T(8,128)(2,1)} %constant.40.clone.fwd_ref) | copy-start | bytes 786436
  1.6 8.3 %collective-permute-start = (bf16[2,32,2048]{2,1,0:T(8,128)(2,1)S(1)}, bf16[2,32,2048]{2,1,0:T(8,128)(2,1)S(1)}, u32[]{:S(2)}, u32[]{:S(2)}) collective-permute-start(bf16[2,32,2048]{2,1,0:T(8,128)(2,1)S(1)} %shard_map.100.own_ref), channel_id=1, source_target_pairs={{2,0},{4,2},{6,4},{1,3},{3,5},{5,7},{10,8},{12,10},{14,12},{9,11},... | collective-permute-start | bytes 786440 | tf_op jit(solution)/shard_map/ppermute | solution.py:324
  6.6 13.3 %collective-permute-start.2 = (bf16[2,32,2048]{2,1,0:T(8,128)(2,1)S(1)}, bf16[2,32,2048]{2,1,0:T(8,128)(2,1)S(1)}, u32[]{:S(2)}, u32[]{:S(2)}) collective-permute-start(bf16[2,32,2048]{2,1,0:T(8,128)(2,1)S(1)} %shard_map.100.own_ref), channel_id=1, source_target_pairs={{0,2},{2,4},{4,6},{3,1},{5,3},{7,5},{8,10},{10,12},{12,14},{11,9},... | collective-permute-start | bytes 786440 | tf_op jit(solution)/shard_map/ppermute | solution.py:325
  9.8 11.1 %copy-start.6 = (f32[16,128]{1,0:T(8,128)S(1)}, f32[16,128]{1,0:T(8,128)}, u32[]{:S(2)}) copy-start(f32[16,128]{1,0:T(8,128)} %constant.43.clone.wave_ref) | copy-start | bytes 24580
  9.9 11.1 %copy-start.4 = (f32[2,16,128]{2,1,0:T(8,128)S(1)}, f32[2,16,128]{2,1,0:T(8,128)}, u32[]{:S(2)}) copy-start(f32[2,16,128]{2,1,0:T(8,128)} %constant.42.clone.tw_ref.tw_i_ref) | copy-start | bytes 49156
  9.9 11.1 %copy-start.5 = (f32[2,16,128]{2,1,0:T(8,128)S(1)}, f32[2,16,128]{2,1,0:T(8,128)}, u32[]{:S(2)}) copy-start(f32[2,16,128]{2,1,0:T(8,128)} %constant.45.clone.step_ref) | copy-start | bytes 49156
  9.9 11.0 %collective-permute-start.1 = (bf16[2,32,2048]{2,1,0:T(8,128)(2,1)S(1)}, bf16[2,32,2048]{2,1,0:T(8,128)(2,1)S(1)}, u32[]{:S(2)}, u32[]{:S(2)}) collective-permute-start(bf16[2,32,2048]{2,1,0:T(8,128)(2,1)S(1)} %shard_map.101), channel_id=1, source_target_pairs={{0,1},{1,0},{2,3},{3,2},{4,5},{5,4},{6,7},{7,6},{8,9},{9,8},{10,11... | collective-permute-start | bytes 786440 | tf_op jit(solution)/shard_map/ppermute | solution.py:333
  22.8 28.1 %copy-start.3 = (bf16[2,256,256]{2,1,0:T(8,128)(2,1)S(1)}, bf16[2,256,256]{2,1,0:T(8,128)(2,1)}, u32[]{:S(2)}) copy-start(bf16[2,256,256]{2,1,0:T(8,128)(2,1)} %constant.46.clone.fwd_ref) | copy-start | bytes 786436
  22.8 28.1 %copy-start.7 = (f32[2,16,128]{2,1,0:T(8,128)S(1)}, f32[2,16,128]{2,1,0:T(8,128)}, u32[]{:S(2)}) copy-start(f32[2,16,128]{2,1,0:T(8,128)} %constant.47.clone.tw_f_ref) | copy-start | bytes 49156

commit v3 on v2

--- a/solution.py
+++ b/solution.py
@@ -41,7 +41,7 @@
     def split(matrix):
         high = matrix.astype(jnp.bfloat16)
         low = (matrix - high.astype(np.float64)).astype(jnp.bfloat16)
-        return np.stack([np.asarray(high), np.asarray(low)])
+        return np.concatenate([np.asarray(high), np.asarray(low)])
 
     def twiddle(order):
         angle = 2.0 * np.pi * np.arange(COLS)[:, None] * order[None, :] / GRID
@@ -157,42 +157,47 @@
     return out
 
 
-def double_dot(left, table_ref):
-    return jnp.dot(left, table_ref[0], preferred_element_type=jnp.float32) + jnp.dot(
-        left, table_ref[1], preferred_element_type=jnp.float32
-    )
-
-
-def sweep(load, store, first_row, fwd_ref, inv_ref, tw_f_ref, tw_i_ref, wave_ref, own_ref, step_ref, buf, sign, finish=None):
+def matrix_stage(re, im, table_ref):
+    left = jnp.concatenate(
+        [
+            jnp.concatenate([jnp.concatenate([part[g][m] for g in range(GROUPS)], axis=0) for part in (re, im)], axis=1)
+            for m in range(COLS)
+        ],
+        axis=0,
+    ).astype(jnp.bfloat16)
+    left = jnp.concatenate([left, left], axis=1)
+    return jnp.dot(left, table_ref[...], preferred_element_type=jnp.float32)
+
+
+def sweep(load, store, first_row, fwd_ref, inv_ref, tw_f_ref, tw_i_ref, wave_ref, rows_ref, step_ref, sign, finish=None):
+    def parts_of(value, m, g):
+        rows = slice(ROWS * m + 8 * g, ROWS * m + 8 * g + 8)
+        return value[rows, :LANES], value[rows, LANES:]
+
+    re_in, im_in = [], []
     for g in range(GROUPS):
-        rows = slice(8 * g, 8 * g + 8)
         out = dft16([load(g, c) for c in range(COLS)], 1)
-        for m in range(COLS):
+        for m in range(1, COLS):
             re, im = out[m]
-            if m > 0:
-                c, s = tw_f_ref[0, m : m + 1, :], tw_f_ref[1, m : m + 1, :]
-                re, im = re * c + im * s, im * c - re * s
-            buf[m, rows, :LANES] = re
-            buf[m, rows, LANES:] = im
-    spectrum = double_dot(buf[...].reshape(COLS * ROWS, 2 * LANES).astype(jnp.bfloat16), fwd_ref)
-    buf[...] = spectrum.reshape(COLS, ROWS, 2 * LANES)
+            c, s = tw_f_ref[0, m : m + 1, :], tw_f_ref[1, m : m + 1, :]
+            out[m] = (re * c + im * s, im * c - re * s)
+        re_in.append([v[0] for v in out])
+        im_in.append([v[1] for v in out])
+    spectrum = matrix_stage(re_in, im_in, fwd_ref)
     phases = row_phases(first_row, wave_ref[...], step_ref[...], sign)
+    re_in, im_in = [[None] * COLS for _ in range(GROUPS)], [[None] * COLS for _ in range(GROUPS)]
     for m in range(COLS):
-        own_re, own_im = own_ref[0, m], -sign * own_ref[1, m]
+        own_re, own_im = rows_ref[0, m], -sign * rows_ref[1, m]
         for g in range(GROUPS):
-            rows = slice(8 * g, 8 * g + 8)
             row_re, row_im = phases[g][0][m : m + 1, :], phases[g][1][m : m + 1, :]
             f_re, f_im = own_re * row_re - own_im * row_im, own_re * row_im + own_im * row_re
-            re, im = buf[m, rows, :LANES], buf[m, rows, LANES:]
-            buf[m, rows, :LANES] = re * f_re - im * f_im
-            buf[m, rows, LANES:] = re * f_im + im * f_re
-    turned = double_dot(buf[...].reshape(COLS * ROWS, 2 * LANES).astype(jnp.bfloat16), inv_ref)
-    buf[...] = turned.reshape(COLS, ROWS, 2 * LANES)
+            re, im = parts_of(spectrum, m, g)
+            re_in[g][m], im_in[g][m] = re * f_re - im * f_im, re * f_im + im * f_re
+    turned = matrix_stage(re_in, im_in, inv_ref)
     for g in range(GROUPS):
-        rows = slice(8 * g, 8 * g + 8)
         terms = []
         for m in range(COLS):
-            re, im = buf[m, rows, :LANES], buf[m, rows, LANES:]
+            re, im = parts_of(turned, m, g)
             if m > 0:
                 c, s = tw_i_ref[0, m : m + 1, :], tw_i_ref[1, m : m + 1, :]
                 re, im = re * c - im * s, im * c + re * s
@@ -226,25 +231,26 @@
             out_ref[1, rows, cols] = (im * cosine - re * sine).astype(jnp.bfloat16)
 
 
-def message_kernel(own_ref, far_ref, out_ref):
-    for p in range(2):
-        total = own_ref[p].astype(jnp.float32) + far_ref[p].astype(jnp.float32)
-        out_ref[p] = total.astype(jnp.bfloat16)
-
-
-def x_kernel(scalar_ref, own_ref, near_ref, far_ref, across_ref, fwd_ref, inv_ref, tw_ref, wave_ref, rows_ref, step_ref, out_ref, mixed, buf, swept):
+def message_kernel(own_ref, beside_ref, out_ref):
+    re, im = own_ref[0].astype(jnp.float32), own_ref[1].astype(jnp.float32)
+    bre, bim = beside_ref[0].astype(jnp.float32), beside_ref[1].astype(jnp.float32)
+    out_ref[0] = (NEAR[0] * re - NEAR[1] * im + FAR * bre).astype(jnp.bfloat16)
+    out_ref[1] = (NEAR[0] * im + NEAR[1] * re + FAR * bim).astype(jnp.bfloat16)
+
+
+def x_kernel(scalar_ref, own_ref, beside_ref, near_ref, across_ref, fwd_ref, inv_ref, tw_ref, wave_ref, rows_ref, step_ref, out_ref, mixed, swept):
     centre = scalar_ref[1]
     for g in range(2):
         rows = slice(16 * g, 16 * g + 16)
         for c in range(COLS):
             at = slice(LANES * c, LANES * c + LANES)
-            re, im, nre, nim, fre, fim, are, aim = (
+            re, im, bre, bim, nre, nim, are, aim = (
                 ref[p, rows, at].astype(jnp.float32)
-                for ref in (own_ref, near_ref, far_ref, across_ref)
+                for ref in (own_ref, beside_ref, near_ref, across_ref)
                 for p in range(2)
             )
-            mixed[0, rows, at] = centre * re - CENTRE[1] * im + (NEAR[0] * nre - NEAR[1] * nim) + FAR * (fre + are)
-            mixed[1, rows, at] = centre * im + CENTRE[1] * re + (NEAR[0] * nim + NEAR[1] * nre) + FAR * (fim + aim)
+            mixed[0, rows, at] = centre * re - CENTRE[1] * im + (NEAR[0] * bre - NEAR[1] * bim) + (nre + FAR * are)
+            mixed[1, rows, at] = centre * im + CENTRE[1] * re + (NEAR[0] * bim + NEAR[1] * bre) + (nim + FAR * aim)
 
     def load(g, c):
         at = slice(LANES * c, LANES * c + LANES)
@@ -254,7 +260,7 @@
         swept[c, 0, g] = re
         swept[c, 1, g] = im
 
-    sweep(load, store, scalar_ref[0], fwd_ref, inv_ref, tw_ref, tw_ref, wave_ref, rows_ref, step_ref, buf, 1.0)
+    sweep(load, store, scalar_ref[0], fwd_ref, inv_ref, tw_ref, tw_ref, wave_ref, rows_ref, step_ref, 1.0)
     for c in range(COLS):
         re = swap_blocks([swept[c, 0, g] for g in range(GROUPS)])
         im = swap_blocks([swept[c, 1, g] for g in range(GROUPS)])
@@ -262,7 +268,7 @@
             out_ref[4 * c + q] = jnp.concatenate([re[q], im[q]], axis=0).astype(jnp.bfloat16)
 
 
-def y_kernel(scalar_ref, in_ref, fwd_ref, inv_ref, tw_f_ref, tw_i_ref, wave_ref, rows_ref, step_ref, out_hbm, field, buf, out_ref, sems):
+def y_kernel(scalar_ref, in_ref, fwd_ref, inv_ref, tw_f_ref, tw_i_ref, wave_ref, rows_ref, step_ref, out_hbm, field, out_ref, sems):
     for s in range(4):
         block = in_ref[16 * s : 16 * s + 16].astype(jnp.float32)
         for p in range(2):
@@ -289,7 +295,7 @@
             copies.append(pltpu.make_async_copy(out_ref.at[p, rows], out_hbm.at[p, 0, rows], sems.at[g, p]))
             copies[-1].start()
 
-    sweep(load, store, scalar_ref[0], fwd_ref, inv_ref, tw_f_ref, tw_i_ref, wave_ref, rows_ref, step_ref, buf, -1.0, send)
+    sweep(load, store, scalar_ref[0], fwd_ref, inv_ref, tw_f_ref, tw_i_ref, wave_ref, rows_ref, step_ref, -1.0, send)
     for copy in copies:
         copy.wait()
 
@@ -319,9 +325,9 @@
         ],
         compiler_params=PARAMS,
     )(pltpu.with_memory_space_constraint(wave, pltpu.HBM), pltpu.with_memory_space_constraint(potential, pltpu.HBM))
-    outward = [(i, i - 2) for i in (2, 4, 6)] + [(i, i + 2) for i in (1, 3, 5)]
+    outward = [(i, i - 1) for i in (2, 4, 6)] + [(i, i + 1) for i in (1, 3, 5)]
     inward = [(i, i + 2) for i in (0, 2, 4)] + [(i, i - 2) for i in (3, 5, 7)]
-    far = lax.ppermute(own, "gz", outward)
+    beside = lax.ppermute(own, "gz", outward)
     across = lax.ppermute(own, "gz", inward)
     message = pl.pallas_call(
         message_kernel,
@@ -329,7 +335,7 @@
         in_specs=[VMEM, VMEM],
         out_specs=VMEM,
         compiler_params=PARAMS,
-    )(own, far)
+    )(own, beside)
     near = lax.ppermute(message, "gz", [(i, i ^ 1) for i in range(8)])
     chunks = pl.pallas_call(
         x_kernel,
@@ -338,11 +344,10 @@
         out_specs=VMEM,
         scratch_shapes=[
             pltpu.VMEM((2, ROWS, GRID), f32),
-            pltpu.VMEM((COLS, ROWS, 2 * LANES), f32),
             pltpu.VMEM((COLS, 2, GROUPS, 8, LANES), f32),
         ],
         compiler_params=PARAMS,
-    )(scalars, own, near, far, across, t["fwd_x"], t["inv"], t["tw_x"], t["wavenum"], t["own"], t["step8"])
+    )(scalars, own, beside, near, across, t["fwd_x"], t["inv"], t["tw_x"], t["wavenum"], t["own"], t["step8"])
     chunks = lax.all_to_all(chunks, "wa", 0, 0, tiled=True)
     return pl.pallas_call(
         y_kernel,
@@ -351,7 +356,6 @@
         out_specs=HBM,
         scratch_shapes=[
             pltpu.VMEM((2, ROWS, GRID), f32),
-            pltpu.VMEM((COLS, ROWS, 2 * LANES), f32),
             pltpu.VMEM((2, ROWS, GRID), f32),
             pltpu.SemaphoreType.DMA((GROUPS, 2)),
         ],

time: 54.3 us -> 53.1 us (0.978)
  starting transfers between devices: 16.1 us -> 8.73 us
  blocking collectives: 28.1 us -> 33 us
  waiting for transfers between devices: 3.03 us -> 4.26 us
    ppermute x1, starting transfers between devices: 9.87 us -> 1.92 us  [on_device(): near = lax.ppermute(message, 'gz', [(i, i ^ 1) for i in range(8)])]
    all_to_all x1, blocking collectives: 28.1 us -> 33 us  [on_device(): chunks = lax.all_to_all(chunks, 'wa', 0, 0, tiled=True)]
    ppermute x1, waiting for transfers between devices: 0.01 us -> 1.52 us  [on_device(): across = lax.ppermute(own, 'gz', inward)]
    ppermute x1, waiting for transfers between devices: 1.05 us -> 0.01 us  [on_device(): near = lax.ppermute(message, 'gz', [(i, i ^ 1) for i in range(8)])]
    ppermute x1, waiting for transfers between devices: 1.98 us -> 2.74 us  [on_device(): beside = lax.ppermute(own, 'gz', outward)]
    ppermute x1, starting transfers between devices: 4.97 us -> 5.52 us  [on_device(): beside = lax.ppermute(own, 'gz', outward)]
where the time goes in v3:
time: 53.1 us; the launch traced here: 52.2 us
  blocking collectives  33 us (62%)
  starting transfers between devices  8.73 us (16%)
  Pallas kernels  5.92 us (11%)
  waiting for transfers between devices  4.26 us (8%)
    all_to_all x1, blocking collectives, on_device(): chunks = lax.all_to_all(chunks, 'wa', 0, 0, tiled=True)  33 us
    ppermute x1, starting transfers between devices, on_device(): beside = lax.ppermute(own, 'gz', outward)  5.52 us
    ppermute x1, waiting for transfers between devices, on_device(): beside = lax.ppermute(own, 'gz', outward)  2.74 us
    pallas_call x1, Pallas kernels, on_device(): pl.pallas_call(y_kernel, out_shape=jax.ShapeDtypeStruct((2, 1, ROWS, GRID...  2.44 us
    ppermute x1, starting transfers between devices, on_device(): near = lax.ppermute(message, 'gz', [(i, i ^ 1) for i in range(8)])  1.92 us
    pallas_call x1, Pallas kernels, on_device(): pl.pallas_call(x_kernel, out_shape=jax.ShapeDtypeStruct((PARTS_WA, 16, LA...  1.79 us
    pallas_call x1, Pallas kernels, on_device(): pl.pallas_call(potential_kernel, out_shape=jax.ShapeDtypeStruct((2, ROWS,...  1.54 us
    ppermute x1, waiting for transfers between devices, on_device(): across = lax.ppermute(own, 'gz', inward)  1.52 us
  transfers between devices with their start and end apart: 3, of which 2 were waited for; matrix products, arithmetic and copies ran while one was open for 0% of the time, Pallas kernels for 0%

profile of v3, /device:TPU:1, one launch (start us, length us, event | category | flops | bytes accessed | tf_op | source)
XLA Modules:
  0.0 52.2 jit_solution(17445368046739095926)
XLA Ops:
  0.0 1.5 %shard_map.100.own_ref = bf16[2,32,2048]{2,1,0:T(8,128)(2,1)S(1)} custom-call(f32[2,1,32,2048]{3,2,1,0:T(8,128)} %wave_hbm.1, f32[1,32,2048]{2,1,0:T(8,128)} %potential_hbm.1), custom_call_target="tpu_custom_call" | custom-call | tf_op jit(solution)/shard_map/pallas_call | solution.py:316
  1.5 0.0 copy-start
  1.6 0.0 copy-start.1
  1.6 0.0 copy-start.2
  1.6 5.5 %collective-permute-start = (bf16[2,32,2048]{2,1,0:T(8,128)(2,1)S(1)}, bf16[2,32,2048]{2,1,0:T(8,128)(2,1)S(1)}, u32[]{:S(2)}, u32[]{:S(2)}) collective-permute-start(bf16[2,32,2048]{2,1,0:T(8,128)(2,1)S(1)} %shard_map.100.own_ref), channel_id=1, source_target_pairs={{2,1},{4,3},{6,5},{1,2},{3,4},{5,6},{10,9},{12,11},{14,13},{9,10},... | collective-permute-start | bytes 786440 | tf_op jit(solution)/shard_map/ppermute | solution.py:330
  7.1 1.3 %collective-permute-start.2 = (bf16[2,32,2048]{2,1,0:T(8,128)(2,1)S(1)}, bf16[2,32,2048]{2,1,0:T(8,128)(2,1)S(1)}, u32[]{:S(2)}, u32[]{:S(2)}) collective-permute-start(bf16[2,32,2048]{2,1,0:T(8,128)(2,1)S(1)} %shard_map.100.own_ref), channel_id=1, source_target_pairs={{0,2},{2,4},{4,6},{3,1},{5,3},{7,5},{8,10},{10,12},{12,14},{11,9},... | collective-permute-start | bytes 786440 | tf_op jit(solution)/shard_map/ppermute | solution.py:331
  8.4 2.7 %collective-permute-done.beside_ref = bf16[2,32,2048]{2,1,0:T(8,128)(2,1)S(1)} collective-permute-done((bf16[2,32,2048]{2,1,0:T(8,128)(2,1)S(1)}, bf16[2,32,2048]{2,1,0:T(8,128)(2,1)S(1)}, u32[]{:S(2)}, u32[]{:S(2)}) %collective-permute-start) | collective-permute-done | bytes 262176 | tf_op jit(solution)/shard_map/ppermute | solution.py:330
  11.2 0.1 shard_map.101
  11.3 0.0 copy-start.4
  11.3 0.0 copy-start.5
  11.3 1.9 %collective-permute-start.1 = (bf16[2,32,2048]{2,1,0:T(8,128)(2,1)S(1)}, bf16[2,32,2048]{2,1,0:T(8,128)(2,1)S(1)}, u32[]{:S(2)}, u32[]{:S(2)}) collective-permute-start(bf16[2,32,2048]{2,1,0:T(8,128)(2,1)S(1)} %shard_map.101), channel_id=1, source_target_pairs={{0,1},{1,0},{2,3},{3,2},{4,5},{5,4},{6,7},{7,6},{8,9},{9,8},{10,11... | collective-permute-start | bytes 786440 | tf_op jit(solution)/shard_map/ppermute | solution.py:339
  13.3 0.1 pad_maximum_fusion.scalar_ref
  13.3 1.5 %collective-permute-done.2.across_ref = bf16[2,32,2048]{2,1,0:T(8,128)(2,1)S(1)} collective-permute-done((bf16[2,32,2048]{2,1,0:T(8,128)(2,1)S(1)}, bf16[2,32,2048]{2,1,0:T(8,128)(2,1)S(1)}, u32[]{:S(2)}, u32[]{:S(2)}) %collective-permute-start.2) | collective-permute-done | bytes 262176 | tf_op jit(solution)/shard_map/ppermute | solution.py:331
  14.9 0.0 collective-permute-done.1.near_ref
  14.9 0.0 copy-done
  14.9 0.0 copy-done.1
  14.9 0.0 copy-done.2
  14.9 0.0 copy-done.6
  14.9 1.8 %shard_map.102 = bf16[64,16,128]{2,1,0:T(8,128)(2,1)S(1)} custom-call(f32[2]{0:T(128)S(1)} %pad_maximum_fusion.scalar_ref, bf16[2,32,2048]{2,1,0:T(8,128)(2,1)S(1)} %shard_map.100.own_ref, bf16[2,32,2048]{2,1,0:T(8,128)(2,1)S(1)} %collective-permute-done.beside_ref, bf16[2,32,2048]{2,1,0:T(8,128)(2,1)S(1)} %collective-permute-done.1.near_ref, ...), custom_call_target="tpu_custom_call" | custom-call | tf_op jit(solution)/shard_map/pallas_call | solution.py:340
  16.7 0.0 copy-start.3
  16.7 0.0 copy-start.7
  16.7 33.0 %all_to_all.5.in_ref = bf16[64,16,128]{2,1,0:T(8,128)(2,1)S(1)} all-to-all(bf16[64,16,128]{2,1,0:T(8,128)(2,1)S(1)} %shard_map.102), channel_id=1, replica_groups=mesh['wa'=64,'gz'=8] {'wa'}, dimensions={0} | all-to-all | bytes 524288 | tf_op jit(solution)/shard_map/all_to_all | solution.py:351
  49.7 0.0 copy-done.3
  49.7 2.4 %shard_map.103 = f32[2,1,32,2048]{3,2,1,0:T(8,128)} custom-call(f32[2]{0:T(128)S(1)} %pad_maximum_fusion.scalar_ref, bf16[64,16,128]{2,1,0:T(8,128)(2,1)S(1)} %all_to_all.5.in_ref, bf16[512,256]{1,0:T(8,128)(2,1)S(1)} %copy-done.3, bf16[512,256]{1,0:T(8,128)(2,1)S(1)} %copy-done, f32[2,16,128]{2,1,0:T(8,128)S(1)} %copy-done.7, f32[2,16,128]{2,1,0:T(8,128)S(1)} %copy-done.4, ...), custom_call_target="tpu_custom_call" | custom-call | tf_op jit(solution)/shard_map/pallas_call | solution.py:352
  (4 shorter events, 0.0 us)
Async XLA Ops:
  1.5 13.3 %copy-start = (bf16[512,256]{1,0:T(8,128)(2,1)S(1)}, bf16[512,256]{1,0:T(8,128)(2,1)}, u32[]{:S(2)}) copy-start(bf16[512,256]{1,0:T(8,128)(2,1)} %constant.41.clone.inv_ref) | copy-start | bytes 786436
  1.6 13.3 %copy-start.1 = (f32[2,16,8,128]{3,2,1,0:T(8,128)S(1)}, f32[2,16,8,128]{3,2,1,0:T(8,128)}, u32[]{:S(2)}) copy-start(f32[2,16,8,128]{3,2,1,0:T(8,128)} %constant.44.clone.rows_ref) | copy-start | bytes 393220
  1.6 13.3 %copy-start.2 = (bf16[512,256]{1,0:T(8,128)(2,1)S(1)}, bf16[512,256]{1,0:T(8,128)(2,1)}, u32[]{:S(2)}) copy-start(bf16[512,256]{1,0:T(8,128)(2,1)} %constant.40.clone.fwd_ref) | copy-start | bytes 786436
  1.6 9.6 %collective-permute-start = (bf16[2,32,2048]{2,1,0:T(8,128)(2,1)S(1)}, bf16[2,32,2048]{2,1,0:T(8,128)(2,1)S(1)}, u32[]{:S(2)}, u32[]{:S(2)}) collective-permute-start(bf16[2,32,2048]{2,1,0:T(8,128)(2,1)S(1)} %shard_map.100.own_ref), channel_id=1, source_target_pairs={{2,1},{4,3},{6,5},{1,2},{3,4},{5,6},{10,9},{12,11},{14,13},{9,10},... | collective-permute-start | bytes 786440 | tf_op jit(solution)/shard_map/ppermute | solution.py:330
  7.1 7.8 %collective-permute-start.2 = (bf16[2,32,2048]{2,1,0:T(8,128)(2,1)S(1)}, bf16[2,32,2048]{2,1,0:T(8,128)(2,1)S(1)}, u32[]{:S(2)}, u32[]{:S(2)}) collective-permute-start(bf16[2,32,2048]{2,1,0:T(8,128)(2,1)S(1)} %shard_map.100.own_ref), channel_id=1, source_target_pairs={{0,2},{2,4},{4,6},{3,1},{5,3},{7,5},{8,10},{10,12},{12,14},{11,9},... | collective-permute-start | bytes 786440 | tf_op jit(solution)/shard_map/ppermute | solution.py:331
  11.2 3.7 %copy-start.6 = (f32[16,128]{1,0:T(8,128)S(1)}, f32[16,128]{1,0:T(8,128)}, u32[]{:S(2)}) copy-start(f32[16,128]{1,0:T(8,128)} %constant.43.clone.wave_ref) | copy-start | bytes 24580
  11.3 3.6 %copy-start.4 = (f32[2,16,128]{2,1,0:T(8,128)S(1)}, f32[2,16,128]{2,1,0:T(8,128)}, u32[]{:S(2)}) copy-start(f32[2,16,128]{2,1,0:T(8,128)} %constant.42.clone.tw_ref.tw_i_ref) | copy-start | bytes 49156
  11.3 3.6 %copy-start.5 = (f32[2,16,128]{2,1,0:T(8,128)S(1)}, f32[2,16,128]{2,1,0:T(8,128)}, u32[]{:S(2)}) copy-start(f32[2,16,128]{2,1,0:T(8,128)} %constant.45.clone.step_ref) | copy-start | bytes 49156
  11.3 3.5 %collective-permute-start.1 = (bf16[2,32,2048]{2,1,0:T(8,128)(2,1)S(1)}, bf16[2,32,2048]{2,1,0:T(8,128)(2,1)S(1)}, u32[]{:S(2)}, u32[]{:S(2)}) collective-permute-start(bf16[2,32,2048]{2,1,0:T(8,128)(2,1)S(1)} %shard_map.101), channel_id=1, source_target_pairs={{0,1},{1,0},{2,3},{3,2},{4,5},{5,4},{6,7},{7,6},{8,9},{9,8},{10,11... | collective-permute-start | bytes 786440 | tf_op jit(solution)/shard_map/ppermute | solution.py:339
  16.7 33.0 %copy-start.3 = (bf16[512,256]{1,0:T(8,128)(2,1)S(1)}, bf16[512,256]{1,0:T(8,128)(2,1)}, u32[]{:S(2)}) copy-start(bf16[512,256]{1,0:T(8,128)(2,1)} %constant.46.clone.fwd_ref) | copy-start | bytes 786436
  16.7 33.0 %copy-start.7 = (f32[2,16,128]{2,1,0:T(8,128)S(1)}, f32[2,16,128]{2,1,0:T(8,128)}, u32[]{:S(2)}) copy-start(f32[2,16,128]{2,1,0:T(8,128)} %constant.47.clone.tw_f_ref) | copy-start | bytes 49156

commit v4 on v3

--- a/solution.py
+++ b/solution.py
@@ -69,25 +69,19 @@
     }
 
 
+SINE = (6.283182621002197, -41.34142303466797, 81.59618377685547, -76.5801010131836, 41.205387115478516, -12.271249771118164)
+COSINE = (0.9999992251396179, -19.738983154296875, 64.92872619628906, -85.27239227294922, 58.794029235839844, -21.076766967773438)
+
+
 def sincos(angle):
-    turns = jnp.floor(angle * (2.0 / math.pi) + 0.5)
-    rest = angle - turns * 1.5703125
-    rest = rest - turns * 4.837512969970703e-4
-    rest = rest - turns * 7.54978995489188e-8
+    turns = angle * (0.5 / math.pi)
+    rest = turns - jnp.floor(turns + 0.5)
     square = rest * rest
-    sine = rest + rest * square * (
-        -1.6666654611e-1 + square * (8.3321608736e-3 - square * 1.9515295891e-4)
-    )
-    cosine = 1.0 - 0.5 * square + square * square * (
-        4.166664568298827e-2 + square * (-1.388731625493765e-3 + square * 2.443315711809948e-5)
-    )
-    quadrant = turns.astype(jnp.int32)
-    swapped = (quadrant & 1) == 1
-    sin_out = jnp.where(swapped, cosine, sine)
-    cos_out = jnp.where(swapped, sine, cosine)
-    sin_out = jnp.where((quadrant & 2) == 2, -sin_out, sin_out)
-    cos_out = jnp.where(((quadrant + 1) & 2) == 2, -cos_out, cos_out)
-    return sin_out, cos_out
+    sine, cosine = SINE[-1], COSINE[-1]
+    for first, second in zip(SINE[-2::-1], COSINE[-2::-1]):
+        sine = sine * square + first
+        cosine = cosine * square + second
+    return sine * rest, cosine
 
 
 def dft4(v, sign):
@@ -238,29 +232,34 @@
     out_ref[1] = (NEAR[0] * im + NEAR[1] * re + FAR * bim).astype(jnp.bfloat16)
 
 
-def x_kernel(scalar_ref, own_ref, beside_ref, near_ref, across_ref, fwd_ref, inv_ref, tw_ref, wave_ref, rows_ref, step_ref, out_ref, mixed, swept):
-    centre = scalar_ref[1]
+def mix_kernel(scalar_ref, own_ref, beside_ref, across_ref, out_ref):
+    centre = scalar_ref[1:2, :]
     for g in range(2):
         rows = slice(16 * g, 16 * g + 16)
         for c in range(COLS):
             at = slice(LANES * c, LANES * c + LANES)
-            re, im, bre, bim, nre, nim, are, aim = (
-                ref[p, rows, at].astype(jnp.float32)
-                for ref in (own_ref, beside_ref, near_ref, across_ref)
-                for p in range(2)
+            re, im, bre, bim, are, aim = (
+                ref[p, rows, at].astype(jnp.float32) for ref in (own_ref, beside_ref, across_ref) for p in range(2)
             )
-            mixed[0, rows, at] = centre * re - CENTRE[1] * im + (NEAR[0] * bre - NEAR[1] * bim) + (nre + FAR * are)
-            mixed[1, rows, at] = centre * im + CENTRE[1] * re + (NEAR[0] * bim + NEAR[1] * bre) + (nim + FAR * aim)
+            out_ref[0, rows, at] = centre * re - CENTRE[1] * im + (NEAR[0] * bre - NEAR[1] * bim) + FAR * are
+            out_ref[1, rows, at] = centre * im + CENTRE[1] * re + (NEAR[0] * bim + NEAR[1] * bre) + FAR * aim
+
+
+def x_kernel(scalar_ref, mixed_ref, near_ref, fwd_ref, inv_ref, tw_ref, wave_ref, rows_ref, step_ref, out_ref, swept):
+    pairs = {}
 
     def load(g, c):
         at = slice(LANES * c, LANES * c + LANES)
-        return mixed[0, 8 * g : 8 * g + 8, at], mixed[1, 8 * g : 8 * g + 8, at]
+        if g % 2 == 0:
+            pairs[c] = near_ref[:, 8 * g : 8 * g + 16, at].astype(jnp.float32)
+        rows = slice(8 * g, 8 * g + 8)
+        return tuple(mixed_ref[p, rows, at] + pairs[c][p, 8 * (g % 2) : 8 * (g % 2) + 8] for p in range(2))
 
     def store(g, c, re, im):
         swept[c, 0, g] = re
         swept[c, 1, g] = im
 
-    sweep(load, store, scalar_ref[0], fwd_ref, inv_ref, tw_ref, tw_ref, wave_ref, rows_ref, step_ref, 1.0)
+    sweep(load, store, scalar_ref[0:1, :], fwd_ref, inv_ref, tw_ref, tw_ref, wave_ref, rows_ref, step_ref, 1.0)
     for c in range(COLS):
         re = swap_blocks([swept[c, 0, g] for g in range(GROUPS)])
         im = swap_blocks([swept[c, 1, g] for g in range(GROUPS)])
@@ -295,12 +294,11 @@
             copies.append(pltpu.make_async_copy(out_ref.at[p, rows], out_hbm.at[p, 0, rows], sems.at[g, p]))
             copies[-1].start()
 
-    sweep(load, store, scalar_ref[0], fwd_ref, inv_ref, tw_f_ref, tw_i_ref, wave_ref, rows_ref, step_ref, -1.0, send)
+    sweep(load, store, scalar_ref[0:1, :], fwd_ref, inv_ref, tw_f_ref, tw_i_ref, wave_ref, rows_ref, step_ref, -1.0, send)
     for copy in copies:
         copy.wait()
 
 
-SMEM = pl.BlockSpec(memory_space=pltpu.SMEM)
 HBM = pl.BlockSpec(memory_space=pltpu.HBM)
 VMEM = pl.BlockSpec(memory_space=pltpu.VMEM)
 PARAMS = pltpu.CompilerParams(vmem_limit_bytes=48 * 1024 * 1024)
@@ -313,6 +311,7 @@
     plane = lax.axis_index("gz")
     edge = (plane == 0) | (plane == 7)
     scalars = jnp.stack([row_base.astype(f32) * spacing, jnp.where(edge, CENTRE_EDGE, CENTRE[0])])
+    scalars = jnp.broadcast_to(scalars[:, None], (2, LANES))
     own = pl.pallas_call(
         potential_kernel,
         out_shape=jax.ShapeDtypeStruct((2, ROWS, GRID), bf16),
@@ -337,22 +336,28 @@
         compiler_params=PARAMS,
     )(own, beside)
     near = lax.ppermute(message, "gz", [(i, i ^ 1) for i in range(8)])
+    mixed = pl.pallas_call(
+        mix_kernel,
+        out_shape=jax.ShapeDtypeStruct((2, ROWS, GRID), f32),
+        in_specs=[VMEM] * 4,
+        out_specs=VMEM,
+        compiler_params=PARAMS,
+    )(scalars, own, beside, across)
     chunks = pl.pallas_call(
         x_kernel,
         out_shape=jax.ShapeDtypeStruct((PARTS_WA, 16, LANES), bf16),
-        in_specs=[SMEM] + [VMEM] * 10,
+        in_specs=[VMEM] * 9,
         out_specs=VMEM,
         scratch_shapes=[
-            pltpu.VMEM((2, ROWS, GRID), f32),
             pltpu.VMEM((COLS, 2, GROUPS, 8, LANES), f32),
         ],
         compiler_params=PARAMS,
-    )(scalars, own, beside, near, across, t["fwd_x"], t["inv"], t["tw_x"], t["wavenum"], t["own"], t["step8"])
+    )(scalars, mixed, near, t["fwd_x"], t["inv"], t["tw_x"], t["wavenum"], t["own"], t["step8"])
     chunks = lax.all_to_all(chunks, "wa", 0, 0, tiled=True)
     return pl.pallas_call(
         y_kernel,
         out_shape=jax.ShapeDtypeStruct((2, 1, ROWS, GRID), f32),
-        in_specs=[SMEM] + [VMEM] * 8,
+        in_specs=[VMEM] * 9,
         out_specs=HBM,
         scratch_shapes=[
             pltpu.VMEM((2, ROWS, GRID), f32),

time: 53.1 us -> 51.8 us (0.976); the launches traced: 52.2 us -> 51.5 us
  Pallas kernels: 5.92 us -> 4.71 us
  local copies, waits for them, and re-layouts: 0.05 us -> 0.94 us
    unnamed x16, local copies, waits for them, and re-layouts: 0.05 us -> 0.87 us
    pallas_call x1, Pallas kernels: 1.79 us -> 1.04 us  [on_device(): pl.pallas_call(x_kernel, out_shape=jax.ShapeDtypeStruct((PARTS_WA, 16, LA...]
    pallas_call x1, Pallas kernels: 2.44 us -> 1.91 us  [on_device(): pl.pallas_call(y_kernel, out_shape=jax.ShapeDtypeStruct((2, 1, ROWS, GRID...]
  transfers between devices with their start and end apart: 3 -> 3, of which waited for: 2 -> 2; matrix products, arithmetic and copies ran while one was open for 0% -> 0% of each run, Pallas kernels for 0% -> 1%
where the time goes in v4:
time: 51.8 us; the launch traced here: 51.5 us
  blocking collectives  32.8 us (63%)
  starting transfers between devices  8.6 us (17%)
  Pallas kernels  4.71 us (9%)
  waiting for transfers between devices  4.29 us (8%)
  local copies, waits for them, and re-layouts  0.94 us (2%)
    all_to_all x1, blocking collectives, on_device(): chunks = lax.all_to_all(chunks, 'wa', 0, 0, tiled=True)  32.8 us
    ppermute x1, starting transfers between devices, on_device(): beside = lax.ppermute(own, 'gz', outward)  5.39 us
    ppermute x1, waiting for transfers between devices, on_device(): beside = lax.ppermute(own, 'gz', outward)  2.74 us
    ppermute x1, starting transfers between devices, on_device(): near = lax.ppermute(message, 'gz', [(i, i ^ 1) for i in range(8)])  1.92 us
    pallas_call x1, Pallas kernels, on_device(): pl.pallas_call(y_kernel, out_shape=jax.ShapeDtypeStruct((2, 1, ROWS, GRID...  1.91 us
    ppermute x1, waiting for transfers between devices, on_device(): across = lax.ppermute(own, 'gz', inward)  1.54 us
    pallas_call x1, Pallas kernels, on_device(): pl.pallas_call(potential_kernel, out_shape=jax.ShapeDtypeStruct((2, ROWS,...  1.4 us
    ppermute x1, starting transfers between devices, on_device(): across = lax.ppermute(own, 'gz', inward)  1.29 us
  transfers between devices with their start and end apart: 3, of which 2 were waited for; matrix products, arithmetic and copies ran while one was open for 0% of the time, Pallas kernels for 1%

profile of v4, /device:TPU:1, one launch (start us, length us, event | category | flops | bytes accessed | tf_op | source)
XLA Modules:
  0.0 51.5 jit_solution(16734024560046827830)
XLA Ops:
  0.0 1.4 %shard_map.100.own_ref = bf16[2,32,2048]{2,1,0:T(8,128)(2,1)S(1)} custom-call(f32[2,1,32,2048]{3,2,1,0:T(8,128)} %wave_hbm.1, f32[1,32,2048]{2,1,0:T(8,128)} %potential_hbm.1), custom_call_target="tpu_custom_call" | custom-call | tf_op jit(solution)/shard_map/pallas_call | solution.py:315
  1.4 5.4 %collective-permute-start = (bf16[2,32,2048]{2,1,0:T(8,128)(2,1)S(1)}, bf16[2,32,2048]{2,1,0:T(8,128)(2,1)S(1)}, u32[]{:S(2)}, u32[]{:S(2)}) collective-permute-start(bf16[2,32,2048]{2,1,0:T(8,128)(2,1)S(1)} %shard_map.100.own_ref), channel_id=1, source_target_pairs={{2,1},{4,3},{6,5},{1,2},{3,4},{5,6},{10,9},{12,11},{14,13},{9,10},... | collective-permute-start | bytes 786440 | tf_op jit(solution)/shard_map/ppermute | solution.py:329
  6.8 1.3 %collective-permute-start.1 = (bf16[2,32,2048]{2,1,0:T(8,128)(2,1)S(1)}, bf16[2,32,2048]{2,1,0:T(8,128)(2,1)S(1)}, u32[]{:S(2)}, u32[]{:S(2)}) collective-permute-start(bf16[2,32,2048]{2,1,0:T(8,128)(2,1)S(1)} %shard_map.100.own_ref), channel_id=1, source_target_pairs={{0,2},{2,4},{4,6},{3,1},{5,3},{7,5},{8,10},{10,12},{12,14},{11,9},... | collective-permute-start | bytes 786440 | tf_op jit(solution)/shard_map/ppermute | solution.py:330
  8.1 2.7 %collective-permute-done.beside_ref = bf16[2,32,2048]{2,1,0:T(8,128)(2,1)S(1)} collective-permute-done((bf16[2,32,2048]{2,1,0:T(8,128)(2,1)S(1)}, bf16[2,32,2048]{2,1,0:T(8,128)(2,1)S(1)}, u32[]{:S(2)}, u32[]{:S(2)}) %collective-permute-start) | collective-permute-done | bytes 262176 | tf_op jit(solution)/shard_map/ppermute | solution.py:329
  10.9 0.1 shard_map.102
  11.0 1.9 %collective-permute-start.2 = (bf16[2,32,2048]{2,1,0:T(8,128)(2,1)S(1)}, bf16[2,32,2048]{2,1,0:T(8,128)(2,1)S(1)}, u32[]{:S(2)}, u32[]{:S(2)}) collective-permute-start(bf16[2,32,2048]{2,1,0:T(8,128)(2,1)S(1)} %shard_map.102), channel_id=1, source_target_pairs={{0,1},{1,0},{2,3},{3,2},{4,5},{5,4},{6,7},{7,6},{8,9},{9,8},{10,11... | collective-permute-start | bytes 786440 | tf_op jit(solution)/shard_map/ppermute | solution.py:338
  12.9 0.1 pad_maximum_fusion
  13.0 1.5 %collective-permute-done.1.across_ref = bf16[2,32,2048]{2,1,0:T(8,128)(2,1)S(1)} collective-permute-done((bf16[2,32,2048]{2,1,0:T(8,128)(2,1)S(1)}, bf16[2,32,2048]{2,1,0:T(8,128)(2,1)S(1)}, u32[]{:S(2)}, u32[]{:S(2)}) %collective-permute-start.1) | collective-permute-done | bytes 262176 | tf_op jit(solution)/shard_map/ppermute | solution.py:330
  14.6 0.1 broadcast_in_dim.2.scalar_ref
  14.7 0.0 copy-start.6
  14.7 0.2 shard_map.101.mixed_ref
  14.9 0.0 collective-permute-done.2.near_ref
  14.9 0.7 %copy-done = bf16[512,256]{1,0:T(8,128)(2,1)S(1)} copy-done((bf16[512,256]{1,0:T(8,128)(2,1)S(1)}, bf16[512,256]{1,0:T(8,128)(2,1)}, u32[]{:S(2)}) %copy-start) | copy-done | bytes 262168
  15.6 0.0 copy-done.1
  15.6 0.1 copy-done.3
  15.7 0.0 copy-done.4
  15.7 0.0 copy-done.5
  15.7 0.0 copy-done.6
  15.7 1.0 %shard_map.103 = bf16[64,16,128]{2,1,0:T(8,128)(2,1)S(1)} custom-call(f32[2,128]{1,0:T(2,128)S(1)} %broadcast_in_dim.2.scalar_ref, f32[2,32,2048]{2,1,0:T(8,128)S(1)} %shard_map.101.mixed_ref, bf16[2,32,2048]{2,1,0:T(8,128)(2,1)S(1)} %collective-permute-done.2.near_ref, bf16[512,256]{1,0:T(8,128)(2,1)S(1)} %copy-done.3, bf16[512,256]{1,0:T(8,128)(2,1)S(1)} %copy-done, ...), custom_call_target="tpu_custom_call" | custom-call | tf_op jit(solution)/shard_map/pallas_call | solution.py:346
  16.8 0.0 copy-start.2
  16.8 0.0 copy-start.7
  16.8 32.8 %all_to_all.5.in_ref = bf16[64,16,128]{2,1,0:T(8,128)(2,1)S(1)} all-to-all(bf16[64,16,128]{2,1,0:T(8,128)(2,1)S(1)} %shard_map.103), channel_id=1, replica_groups=mesh['wa'=64,'gz'=8] {'wa'}, dimensions={0} | all-to-all | bytes 524288 | tf_op jit(solution)/shard_map/all_to_all | solution.py:356
  49.6 0.0 copy-done.2
  49.6 1.9 %shard_map.104 = f32[2,1,32,2048]{3,2,1,0:T(8,128)} custom-call(f32[2,128]{1,0:T(2,128)S(1)} %broadcast_in_dim.2.scalar_ref, bf16[64,16,128]{2,1,0:T(8,128)(2,1)S(1)} %all_to_all.5.in_ref, bf16[512,256]{1,0:T(8,128)(2,1)S(1)} %copy-done.2, bf16[512,256]{1,0:T(8,128)(2,1)S(1)} %copy-done, f32[2,16,128]{2,1,0:T(8,128)S(1)} %copy-done.7, ...), custom_call_target="tpu_custom_call" | custom-call | tf_op jit(solution)/shard_map/pallas_call | solution.py:357
  (6 shorter events, 0.0 us)
Async XLA Ops:
  1.4 9.4 %collective-permute-start = (bf16[2,32,2048]{2,1,0:T(8,128)(2,1)S(1)}, bf16[2,32,2048]{2,1,0:T(8,128)(2,1)S(1)}, u32[]{:S(2)}, u32[]{:S(2)}) collective-permute-start(bf16[2,32,2048]{2,1,0:T(8,128)(2,1)S(1)} %shard_map.100.own_ref), channel_id=1, source_target_pairs={{2,1},{4,3},{6,5},{1,2},{3,4},{5,6},{10,9},{12,11},{14,13},{9,10},... | collective-permute-start | bytes 786440 | tf_op jit(solution)/shard_map/ppermute | solution.py:329
  6.8 7.8 %collective-permute-start.1 = (bf16[2,32,2048]{2,1,0:T(8,128)(2,1)S(1)}, bf16[2,32,2048]{2,1,0:T(8,128)(2,1)S(1)}, u32[]{:S(2)}, u32[]{:S(2)}) collective-permute-start(bf16[2,32,2048]{2,1,0:T(8,128)(2,1)S(1)} %shard_map.100.own_ref), channel_id=1, source_target_pairs={{0,2},{2,4},{4,6},{3,1},{5,3},{7,5},{8,10},{10,12},{12,14},{11,9},... | collective-permute-start | bytes 786440 | tf_op jit(solution)/shard_map/ppermute | solution.py:330
  11.0 3.9 %collective-permute-start.2 = (bf16[2,32,2048]{2,1,0:T(8,128)(2,1)S(1)}, bf16[2,32,2048]{2,1,0:T(8,128)(2,1)S(1)}, u32[]{:S(2)}, u32[]{:S(2)}) collective-permute-start(bf16[2,32,2048]{2,1,0:T(8,128)(2,1)S(1)} %shard_map.102), channel_id=1, source_target_pairs={{0,1},{1,0},{2,3},{3,2},{4,5},{5,4},{6,7},{7,6},{8,9},{9,8},{10,11... | collective-permute-start | bytes 786440 | tf_op jit(solution)/shard_map/ppermute | solution.py:338
  14.6 1.0 %copy-start = (bf16[512,256]{1,0:T(8,128)(2,1)S(1)}, bf16[512,256]{1,0:T(8,128)(2,1)}, u32[]{:S(2)}) copy-start(bf16[512,256]{1,0:T(8,128)(2,1)} %constant.41.clone.inv_ref) | copy-start | bytes 786436
  14.6 1.0 %copy-start.1 = (f32[2,16,8,128]{3,2,1,0:T(8,128)S(1)}, f32[2,16,8,128]{3,2,1,0:T(8,128)}, u32[]{:S(2)}) copy-start(f32[2,16,8,128]{3,2,1,0:T(8,128)} %constant.44.clone.rows_ref) | copy-start | bytes 393220
  14.6 1.1 %copy-start.3 = (bf16[512,256]{1,0:T(8,128)(2,1)S(1)}, bf16[512,256]{1,0:T(8,128)(2,1)}, u32[]{:S(2)}) copy-start(bf16[512,256]{1,0:T(8,128)(2,1)} %constant.40.clone.fwd_ref) | copy-start | bytes 786436
  14.6 1.1 %copy-start.4 = (f32[2,16,128]{2,1,0:T(8,128)S(1)}, f32[2,16,128]{2,1,0:T(8,128)}, u32[]{:S(2)}) copy-start(f32[2,16,128]{2,1,0:T(8,128)} %constant.42.clone.tw_ref.tw_i_ref) | copy-start | bytes 49156
  14.6 1.1 %copy-start.5 = (f32[2,16,128]{2,1,0:T(8,128)S(1)}, f32[2,16,128]{2,1,0:T(8,128)}, u32[]{:S(2)}) copy-start(f32[2,16,128]{2,1,0:T(8,128)} %constant.45.clone.step_ref) | copy-start | bytes 49156
  14.7 1.1 %copy-start.6 = (f32[16,128]{1,0:T(8,128)S(1)}, f32[16,128]{1,0:T(8,128)}, u32[]{:S(2)}) copy-start(f32[16,128]{1,0:T(8,128)} %constant.43.clone.wave_ref) | copy-start | bytes 24580
  16.8 32.8 %copy-start.2 = (bf16[512,256]{1,0:T(8,128)(2,1)S(1)}, bf16[512,256]{1,0:T(8,128)(2,1)}, u32[]{:S(2)}) copy-start(bf16[512,256]{1,0:T(8,128)(2,1)} %constant.46.clone.fwd_ref) | copy-start | bytes 786436
  16.8 32.8 %copy-start.7 = (f32[2,16,128]{2,1,0:T(8,128)S(1)}, f32[2,16,128]{2,1,0:T(8,128)}, u32[]{:S(2)}) copy-start(f32[2,16,128]{2,1,0:T(8,128)} %constant.47.clone.tw_f_ref) | copy-start | bytes 49156

commit v5 on v4

--- a/solution.py
+++ b/solution.py
@@ -29,7 +29,7 @@
 
 def tables():
     lane = np.arange(LANES)
-    turned_lane = 32 * ((lane // 8) % 4) + 8 * (lane // 32) + lane % 8
+    turned_lane = 32 * ((lane // 16) % 4) + 16 * (lane // 64) + lane % 16
     scale = 1.0 / math.sqrt(GRID)
 
     def matrices(order):
@@ -61,12 +61,12 @@
         "fwd_x": split(matrices(lane)),
         "fwd_y": split(matrices(turned_lane)),
         "inv": backward,
-        "tw_x": twiddle(lane),
-        "tw_y": twiddle(turned_lane),
-        "wavenum": wavenum.astype(np.float32),
+        "small": np.concatenate([twiddle(lane), twiddle(turned_lane), step8, wavenum[None].astype(np.float32)]),
         "own": own,
-        "step8": step8,
     }
+
+
+TWIDDLE, TWIDDLE_TURNED, STEP8, WAVENUM = 0, 2, 4, 6
 
 
 SINE = (6.283182621002197, -41.34142303466797, 81.59618377685547, -76.5801010131836, 41.205387115478516, -12.271249771118164)
@@ -123,19 +123,18 @@
     return out
 
 
+def exchange(first, second, width):
+    upper = (lax.broadcasted_iota(jnp.int32, first.shape, 1) // width) % 2 == 1
+    a = jnp.where(upper, pltpu.roll(second, width, 1), first)
+    b = jnp.where(upper, second, pltpu.roll(first, LANES - width, 1))
+    return a, b
+
+
 def swap_blocks(v):
-    lane = lax.broadcasted_iota(jnp.int32, (8, LANES), 1)
-
-    def stage(first, second, width):
-        upper = (lane // width) % 2 == 1
-        a = jnp.where(upper, pltpu.roll(second, width, 1), first)
-        b = jnp.where(upper, second, pltpu.roll(first, LANES - width, 1))
-        return a, b
-
-    v0, v2 = stage(v[0], v[2], 64)
-    v1, v3 = stage(v[1], v[3], 64)
-    v0, v1 = stage(v0, v1, 32)
-    v2, v3 = stage(v2, v3, 32)
+    v0, v2 = exchange(v[0], v[2], 64)
+    v1, v3 = exchange(v[1], v[3], 64)
+    v0, v1 = exchange(v0, v1, 32)
+    v2, v3 = exchange(v2, v3, 32)
     return [v0, v1, v2, v3]
 
 
@@ -163,7 +162,7 @@
     return jnp.dot(left, table_ref[...], preferred_element_type=jnp.float32)
 
 
-def sweep(load, store, first_row, fwd_ref, inv_ref, tw_f_ref, tw_i_ref, wave_ref, rows_ref, step_ref, sign, finish=None):
+def sweep(load, store, first_row, fwd_ref, inv_ref, small_ref, rows_ref, forward, sign, finish=None):
     def parts_of(value, m, g):
         rows = slice(ROWS * m + 8 * g, ROWS * m + 8 * g + 8)
         return value[rows, :LANES], value[rows, LANES:]
@@ -173,12 +172,12 @@
         out = dft16([load(g, c) for c in range(COLS)], 1)
         for m in range(1, COLS):
             re, im = out[m]
-            c, s = tw_f_ref[0, m : m + 1, :], tw_f_ref[1, m : m + 1, :]
+            c, s = small_ref[forward, m : m + 1, :], small_ref[forward + 1, m : m + 1, :]
             out[m] = (re * c + im * s, im * c - re * s)
         re_in.append([v[0] for v in out])
         im_in.append([v[1] for v in out])
     spectrum = matrix_stage(re_in, im_in, fwd_ref)
-    phases = row_phases(first_row, wave_ref[...], step_ref[...], sign)
+    phases = row_phases(first_row, small_ref[WAVENUM], small_ref[STEP8 : STEP8 + 2], sign)
     re_in, im_in = [[None] * COLS for _ in range(GROUPS)], [[None] * COLS for _ in range(GROUPS)]
     for m in range(COLS):
         own_re, own_im = rows_ref[0, m], -sign * rows_ref[1, m]
@@ -193,7 +192,7 @@
         for m in range(COLS):
             re, im = parts_of(turned, m, g)
             if m > 0:
-                c, s = tw_i_ref[0, m : m + 1, :], tw_i_ref[1, m : m + 1, :]
+                c, s = small_ref[TWIDDLE, m : m + 1, :], small_ref[TWIDDLE + 1, m : m + 1, :]
                 re, im = re * c - im * s, im * c + re * s
             terms.append((re, im))
         for c, (re, im) in enumerate(dft16(terms, -1)):
@@ -208,9 +207,8 @@
     copies = []
     for b, (rows, at) in enumerate(blocks):
         copies.append([
-            pltpu.make_async_copy(wave_hbm.at[0, 0, rows, at], wave_ref.at[0, rows, at], sems.at[b, 0]),
-            pltpu.make_async_copy(wave_hbm.at[1, 0, rows, at], wave_ref.at[1, rows, at], sems.at[b, 1]),
-            pltpu.make_async_copy(potential_hbm.at[0, rows, at], potential_ref.at[rows, at], sems.at[b, 2]),
+            pltpu.make_async_copy(wave_hbm.at[:, 0, rows, at], wave_ref.at[:, rows, at], sems.at[b, 0]),
+            pltpu.make_async_copy(potential_hbm.at[0, rows, at], potential_ref.at[rows, at], sems.at[b, 1]),
         ])
         for copy in copies[-1]:
             copy.start()
@@ -245,7 +243,7 @@
             out_ref[1, rows, at] = centre * im + CENTRE[1] * re + (NEAR[0] * bim + NEAR[1] * bre) + FAR * aim
 
 
-def x_kernel(scalar_ref, mixed_ref, near_ref, fwd_ref, inv_ref, tw_ref, wave_ref, rows_ref, step_ref, out_ref, swept):
+def x_kernel(scalar_ref, mixed_ref, near_ref, fwd_ref, inv_ref, small_ref, rows_ref, out_ref, swept):
     pairs = {}
 
     def load(g, c):
@@ -256,26 +254,26 @@
         return tuple(mixed_ref[p, rows, at] + pairs[c][p, 8 * (g % 2) : 8 * (g % 2) + 8] for p in range(2))
 
     def store(g, c, re, im):
-        swept[c, 0, g] = re
-        swept[c, 1, g] = im
-
-    sweep(load, store, scalar_ref[0:1, :], fwd_ref, inv_ref, tw_ref, tw_ref, wave_ref, rows_ref, step_ref, 1.0)
+        swept[c, 0, 8 * g : 8 * g + 8] = re
+        swept[c, 1, 8 * g : 8 * g + 8] = im
+
+    sweep(load, store, scalar_ref[0:1, :], fwd_ref, inv_ref, small_ref, rows_ref, TWIDDLE, 1.0)
     for c in range(COLS):
-        re = swap_blocks([swept[c, 0, g] for g in range(GROUPS)])
-        im = swap_blocks([swept[c, 1, g] for g in range(GROUPS)])
+        tiles = swap_blocks([swept[c, p, 16 * h : 16 * h + 16] for p in range(2) for h in range(2)])
         for q in range(4):
-            out_ref[4 * c + q] = jnp.concatenate([re[q], im[q]], axis=0).astype(jnp.bfloat16)
-
-
-def y_kernel(scalar_ref, in_ref, fwd_ref, inv_ref, tw_f_ref, tw_i_ref, wave_ref, rows_ref, step_ref, out_hbm, field, out_ref, sems):
-    for s in range(4):
-        block = in_ref[16 * s : 16 * s + 16].astype(jnp.float32)
+            out_ref[4 * c + q] = tiles[q].astype(jnp.bfloat16)
+
+
+def y_kernel(scalar_ref, in_ref, fwd_ref, inv_ref, small_ref, rows_ref, out_hbm, field, out_ref, sems):
+    for s in range(8):
+        flipped = jnp.transpose(in_ref[8 * s : 8 * s + 8].reshape(LANES, LANES)).astype(jnp.float32)
         for p in range(2):
-            flipped = jnp.transpose(block[:, 8 * p : 8 * p + 8, :].reshape(LANES, LANES))
             for x in range(4):
-                parts = swap_blocks([flipped[32 * g + 8 * x : 32 * g + 8 * x + 8] for g in range(4)])
-                for a in range(4):
-                    field[p, 8 * x : 8 * x + 8, LANES * (4 * s + a) : LANES * (4 * s + a + 1)] = parts[a]
+                rows = slice(8 * x, 8 * x + 8)
+                low, high = (flipped[64 * p + 32 * h + 8 * x : 64 * p + 32 * h + 8 * x + 8] for h in range(2))
+                low, high = exchange(low, high, 64)
+                field[p, rows, LANES * (2 * s) : LANES * (2 * s + 1)] = low
+                field[p, rows, LANES * (2 * s + 1) : LANES * (2 * s + 2)] = high
 
     def load(g, c):
         at = slice(LANES * c, LANES * c + LANES)
@@ -294,7 +292,7 @@
             copies.append(pltpu.make_async_copy(out_ref.at[p, rows], out_hbm.at[p, 0, rows], sems.at[g, p]))
             copies[-1].start()
 
-    sweep(load, store, scalar_ref[0:1, :], fwd_ref, inv_ref, tw_f_ref, tw_i_ref, wave_ref, rows_ref, step_ref, -1.0, send)
+    sweep(load, store, scalar_ref[0:1, :], fwd_ref, inv_ref, small_ref, rows_ref, TWIDDLE_TURNED, -1.0, send)
     for copy in copies:
         copy.wait()
 
@@ -320,7 +318,7 @@
         scratch_shapes=[
             pltpu.VMEM((2, ROWS, GRID), f32),
             pltpu.VMEM((ROWS, GRID), f32),
-            pltpu.SemaphoreType.DMA((4, 3)),
+            pltpu.SemaphoreType.DMA((4, 2)),
         ],
         compiler_params=PARAMS,
     )(pltpu.with_memory_space_constraint(wave, pltpu.HBM), pltpu.with_memory_space_constraint(potential, pltpu.HBM))
@@ -346,18 +344,18 @@
     chunks = pl.pallas_call(
         x_kernel,
         out_shape=jax.ShapeDtypeStruct((PARTS_WA, 16, LANES), bf16),
-        in_specs=[VMEM] * 9,
+        in_specs=[VMEM] * 7,
         out_specs=VMEM,
         scratch_shapes=[
-            pltpu.VMEM((COLS, 2, GROUPS, 8, LANES), f32),
+            pltpu.VMEM((COLS, 2, ROWS, LANES), f32),
         ],
         compiler_params=PARAMS,
-    )(scalars, mixed, near, t["fwd_x"], t["inv"], t["tw_x"], t["wavenum"], t["own"], t["step8"])
+    )(scalars, mixed, near, t["fwd_x"], t["inv"], t["small"], t["own"])
     chunks = lax.all_to_all(chunks, "wa", 0, 0, tiled=True)
     return pl.pallas_call(
         y_kernel,
         out_shape=jax.ShapeDtypeStruct((2, 1, ROWS, GRID), f32),
-        in_specs=[VMEM] * 9,
+        in_specs=[VMEM] * 6,
         out_specs=HBM,
         scratch_shapes=[
             pltpu.VMEM((2, ROWS, GRID), f32),
@@ -365,7 +363,7 @@
             pltpu.SemaphoreType.DMA((GROUPS, 2)),
         ],
         compiler_params=PARAMS,
-    )(scalars, chunks, t["fwd_y"], t["inv"], t["tw_y"], t["tw_x"], t["wavenum"], t["own"], t["step8"])
+    )(scalars, chunks, t["fwd_y"], t["inv"], t["small"], t["own"])
 
 
 def solution(mesh):

time: 51.8 us -> 51.6 us (level)
  no operation moved by 1% of the time
where the time goes in v5:
time: 51.6 us; the launch traced here: 51.4 us
  blocking collectives  32.8 us (64%)
  starting transfers between devices  8.6 us (17%)
  Pallas kernels  4.61 us (9%)
  waiting for transfers between devices  4.29 us (8%)
  local copies, waits for them, and re-layouts  0.94 us (2%)
    all_to_all x1, blocking collectives, on_device(): chunks = lax.all_to_all(chunks, 'wa', 0, 0, tiled=True)  32.8 us
    ppermute x1, starting transfers between devices, on_device(): beside = lax.ppermute(own, 'gz', outward)  5.39 us
    ppermute x1, waiting for transfers between devices, on_device(): beside = lax.ppermute(own, 'gz', outward)  2.74 us
    ppermute x1, starting transfers between devices, on_device(): near = lax.ppermute(message, 'gz', [(i, i ^ 1) for i in range(8)])  1.92 us
    pallas_call x1, Pallas kernels, on_device(): pl.pallas_call(y_kernel, out_shape=jax.ShapeDtypeStruct((2, 1, ROWS, GRID...  1.83 us
    ppermute x1, waiting for transfers between devices, on_device(): across = lax.ppermute(own, 'gz', inward)  1.54 us
    pallas_call x1, Pallas kernels, on_device(): pl.pallas_call(potential_kernel, out_shape=jax.ShapeDtypeStruct((2, ROWS,...  1.37 us
    ppermute x1, starting transfers between devices, on_device(): across = lax.ppermute(own, 'gz', inward)  1.29 us
  transfers between devices with their start and end apart: 3, of which 2 were waited for; matrix products, arithmetic and copies ran while one was open for 0% of the time, Pallas kernels for 1%

profile of v5, /device:TPU:1, one launch (start us, length us, event | category | flops | bytes accessed | tf_op | source)
XLA Modules:
  0.0 51.4 jit_solution(6401220136214038910)
XLA Ops:
  0.0 1.4 %shard_map.73.own_ref = bf16[2,32,2048]{2,1,0:T(8,128)(2,1)S(1)} custom-call(f32[2,1,32,2048]{3,2,1,0:T(8,128)} %wave_hbm.1, f32[1,32,2048]{2,1,0:T(8,128)} %potential_hbm.1), custom_call_target="tpu_custom_call" | custom-call | tf_op jit(solution)/shard_map/pallas_call | solution.py:313
  1.4 5.4 %collective-permute-start = (bf16[2,32,2048]{2,1,0:T(8,128)(2,1)S(1)}, bf16[2,32,2048]{2,1,0:T(8,128)(2,1)S(1)}, u32[]{:S(2)}, u32[]{:S(2)}) collective-permute-start(bf16[2,32,2048]{2,1,0:T(8,128)(2,1)S(1)} %shard_map.73.own_ref), channel_id=1, source_target_pairs={{2,1},{4,3},{6,5},{1,2},{3,4},{5,6},{10,9},{12,11},{14,13},{9,10},... | collective-permute-start | bytes 786440 | tf_op jit(solution)/shard_map/ppermute | solution.py:327
  6.8 1.3 %collective-permute-start.1 = (bf16[2,32,2048]{2,1,0:T(8,128)(2,1)S(1)}, bf16[2,32,2048]{2,1,0:T(8,128)(2,1)S(1)}, u32[]{:S(2)}, u32[]{:S(2)}) collective-permute-start(bf16[2,32,2048]{2,1,0:T(8,128)(2,1)S(1)} %shard_map.73.own_ref), channel_id=1, source_target_pairs={{0,2},{2,4},{4,6},{3,1},{5,3},{7,5},{8,10},{10,12},{12,14},{11,9},... | collective-permute-start | bytes 786440 | tf_op jit(solution)/shard_map/ppermute | solution.py:328
  8.1 2.7 %collective-permute-done.beside_ref = bf16[2,32,2048]{2,1,0:T(8,128)(2,1)S(1)} collective-permute-done((bf16[2,32,2048]{2,1,0:T(8,128)(2,1)S(1)}, bf16[2,32,2048]{2,1,0:T(8,128)(2,1)S(1)}, u32[]{:S(2)}, u32[]{:S(2)}) %collective-permute-start) | collective-permute-done | bytes 262176 | tf_op jit(solution)/shard_map/ppermute | solution.py:327
  10.8 0.1 shard_map.75
  11.0 1.9 %collective-permute-start.2 = (bf16[2,32,2048]{2,1,0:T(8,128)(2,1)S(1)}, bf16[2,32,2048]{2,1,0:T(8,128)(2,1)S(1)}, u32[]{:S(2)}, u32[]{:S(2)}) collective-permute-start(bf16[2,32,2048]{2,1,0:T(8,128)(2,1)S(1)} %shard_map.75), channel_id=1, source_target_pairs={{0,1},{1,0},{2,3},{3,2},{4,5},{5,4},{6,7},{7,6},{8,9},{9,8},{10,11... | collective-permute-start | bytes 786440 | tf_op jit(solution)/shard_map/ppermute | solution.py:336
  12.9 0.1 pad_maximum_fusion
  13.0 1.5 %collective-permute-done.1.across_ref = bf16[2,32,2048]{2,1,0:T(8,128)(2,1)S(1)} collective-permute-done((bf16[2,32,2048]{2,1,0:T(8,128)(2,1)S(1)}, bf16[2,32,2048]{2,1,0:T(8,128)(2,1)S(1)}, u32[]{:S(2)}, u32[]{:S(2)}) %collective-permute-start.1) | collective-permute-done | bytes 262176 | tf_op jit(solution)/shard_map/ppermute | solution.py:328
  14.5 0.1 broadcast_in_dim.2.scalar_ref
  14.6 0.0 copy-start
  14.6 0.0 copy-start.1
  14.6 0.0 copy-start.3
  14.6 0.0 copy-start.4
  14.6 0.2 shard_map.74.mixed_ref
  14.8 0.0 collective-permute-done.2.near_ref
  14.8 0.7 %copy-done = bf16[512,256]{1,0:T(8,128)(2,1)S(1)} copy-done((bf16[512,256]{1,0:T(8,128)(2,1)S(1)}, bf16[512,256]{1,0:T(8,128)(2,1)}, u32[]{:S(2)}) %copy-start) | copy-done | bytes 262168
  15.6 0.0 copy-done.1
  15.6 0.1 copy-done.3
  15.7 0.0 copy-done.4
  15.7 1.1 %shard_map.76 = bf16[64,16,128]{2,1,0:T(8,128)(2,1)S(1)} custom-call(f32[2,128]{1,0:T(2,128)S(1)} %broadcast_in_dim.2.scalar_ref, f32[2,32,2048]{2,1,0:T(8,128)S(1)} %shard_map.74.mixed_ref, bf16[2,32,2048]{2,1,0:T(8,128)(2,1)S(1)} %collective-permute-done.2.near_ref, bf16[512,256]{1,0:T(8,128)(2,1)S(1)} %copy-done.3, bf16[512,256]{1,0:T(8,128)(2,1)S(1)} %copy-done, ...), custom_call_target="tpu_custom_call" | custom-call | tf_op jit(solution)/shard_map/pallas_call | solution.py:344
  16.8 0.0 copy-start.2
  16.8 32.8 %all_to_all.5.in_ref = bf16[64,16,128]{2,1,0:T(8,128)(2,1)S(1)} all-to-all(bf16[64,16,128]{2,1,0:T(8,128)(2,1)S(1)} %shard_map.76), channel_id=1, replica_groups=mesh['wa'=64,'gz'=8] {'wa'}, dimensions={0} | all-to-all | bytes 524288 | tf_op jit(solution)/shard_map/all_to_all | solution.py:354
  49.6 0.0 copy-done.2
  49.6 1.8 %shard_map.77 = f32[2,1,32,2048]{3,2,1,0:T(8,128)} custom-call(f32[2,128]{1,0:T(2,128)S(1)} %broadcast_in_dim.2.scalar_ref, bf16[64,16,128]{2,1,0:T(8,128)(2,1)S(1)} %all_to_all.5.in_ref, bf16[512,256]{1,0:T(8,128)(2,1)S(1)} %copy-done.2, bf16[512,256]{1,0:T(8,128)(2,1)S(1)} %copy-done, f32[7,16,128]{2,1,0:T(8,128)S(1)} %copy-done.4, ...), custom_call_target="tpu_custom_call" | custom-call | tf_op jit(solution)/shard_map/pallas_call | solution.py:355
Async XLA Ops:
  1.4 9.4 %collective-permute-start = (bf16[2,32,2048]{2,1,0:T(8,128)(2,1)S(1)}, bf16[2,32,2048]{2,1,0:T(8,128)(2,1)S(1)}, u32[]{:S(2)}, u32[]{:S(2)}) collective-permute-start(bf16[2,32,2048]{2,1,0:T(8,128)(2,1)S(1)} %shard_map.73.own_ref), channel_id=1, source_target_pairs={{2,1},{4,3},{6,5},{1,2},{3,4},{5,6},{10,9},{12,11},{14,13},{9,10},... | collective-permute-start | bytes 786440 | tf_op jit(solution)/shard_map/ppermute | solution.py:327
  6.8 7.8 %collective-permute-start.1 = (bf16[2,32,2048]{2,1,0:T(8,128)(2,1)S(1)}, bf16[2,32,2048]{2,1,0:T(8,128)(2,1)S(1)}, u32[]{:S(2)}, u32[]{:S(2)}) collective-permute-start(bf16[2,32,2048]{2,1,0:T(8,128)(2,1)S(1)} %shard_map.73.own_ref), channel_id=1, source_target_pairs={{0,2},{2,4},{4,6},{3,1},{5,3},{7,5},{8,10},{10,12},{12,14},{11,9},... | collective-permute-start | bytes 786440 | tf_op jit(solution)/shard_map/ppermute | solution.py:328
  11.0 3.9 %collective-permute-start.2 = (bf16[2,32,2048]{2,1,0:T(8,128)(2,1)S(1)}, bf16[2,32,2048]{2,1,0:T(8,128)(2,1)S(1)}, u32[]{:S(2)}, u32[]{:S(2)}) collective-permute-start(bf16[2,32,2048]{2,1,0:T(8,128)(2,1)S(1)} %shard_map.75), channel_id=1, source_target_pairs={{0,1},{1,0},{2,3},{3,2},{4,5},{5,4},{6,7},{7,6},{8,9},{9,8},{10,11... | collective-permute-start | bytes 786440 | tf_op jit(solution)/shard_map/ppermute | solution.py:336
  14.6 1.0 %copy-start = (bf16[512,256]{1,0:T(8,128)(2,1)S(1)}, bf16[512,256]{1,0:T(8,128)(2,1)}, u32[]{:S(2)}) copy-start(bf16[512,256]{1,0:T(8,128)(2,1)} %constant.35.clone.inv_ref) | copy-start | bytes 786436
  14.6 1.0 %copy-start.1 = (f32[2,16,8,128]{3,2,1,0:T(8,128)S(1)}, f32[2,16,8,128]{3,2,1,0:T(8,128)}, u32[]{:S(2)}) copy-start(f32[2,16,8,128]{3,2,1,0:T(8,128)} %constant.37.clone.rows_ref) | copy-start | bytes 393220
  14.6 1.1 %copy-start.3 = (bf16[512,256]{1,0:T(8,128)(2,1)S(1)}, bf16[512,256]{1,0:T(8,128)(2,1)}, u32[]{:S(2)}) copy-start(bf16[512,256]{1,0:T(8,128)(2,1)} %constant.34.clone.fwd_ref) | copy-start | bytes 786436
  14.6 1.1 %copy-start.4 = (f32[7,16,128]{2,1,0:T(8,128)S(1)}, f32[7,16,128]{2,1,0:T(8,128)}, u32[]{:S(2)}) copy-start(f32[7,16,128]{2,1,0:T(8,128)} %constant.36.clone.small_ref) | copy-start | bytes 172036
  16.8 32.8 %copy-start.2 = (bf16[512,256]{1,0:T(8,128)(2,1)S(1)}, bf16[512,256]{1,0:T(8,128)(2,1)}, u32[]{:S(2)}) copy-start(bf16[512,256]{1,0:T(8,128)(2,1)} %constant.38.clone.fwd_ref) | copy-start | bytes 786436

commit v6 on v5

--- a/solution.py
+++ b/solution.py
@@ -153,7 +153,7 @@
 def matrix_stage(re, im, table_ref):
     left = jnp.concatenate(
         [
-            jnp.concatenate([jnp.concatenate([part[g][m] for g in range(GROUPS)], axis=0) for part in (re, im)], axis=1)
+            jnp.concatenate([jnp.concatenate([group[m] for group in part], axis=0) for part in (re, im)], axis=1)
             for m in range(COLS)
         ],
         axis=0,
@@ -163,43 +163,52 @@
 
 
 def sweep(load, store, first_row, fwd_ref, inv_ref, small_ref, rows_ref, forward, sign, finish=None):
-    def parts_of(value, m, g):
-        rows = slice(ROWS * m + 8 * g, ROWS * m + 8 * g + 8)
+    phases = row_phases(first_row, small_ref[WAVENUM], small_ref[STEP8 : STEP8 + 2], sign)
+
+    def parts_of(value, m):
+        rows = slice(8 * m, 8 * m + 8)
         return value[rows, :LANES], value[rows, LANES:]
 
-    re_in, im_in = [], []
+    def first(groups):
+        re_in, im_in = [], []
+        for g in groups:
+            out = dft16([load(g, c) for c in range(COLS)], 1)
+            for m in range(1, COLS):
+                re, im = out[m]
+                c, s = small_ref[forward, m : m + 1, :], small_ref[forward + 1, m : m + 1, :]
+                out[m] = (re * c + im * s, im * c - re * s)
+            re_in.append([v[0] for v in out])
+            im_in.append([v[1] for v in out])
+        return matrix_stage(re_in, im_in, fwd_ref)
+
+    def second(groups, spectrum):
+        re_in, im_in = [[None] * COLS for _ in groups], [[None] * COLS for _ in groups]
+        for m in range(COLS):
+            own_re, own_im = rows_ref[0, m], -sign * rows_ref[1, m]
+            for i, g in enumerate(groups):
+                row_re, row_im = phases[g][0][m : m + 1, :], phases[g][1][m : m + 1, :]
+                f_re, f_im = own_re * row_re - own_im * row_im, own_re * row_im + own_im * row_re
+                re, im = parts_of(spectrum, m)
+                re_in[i][m], im_in[i][m] = re * f_re - im * f_im, re * f_im + im * f_re
+        return matrix_stage(re_in, im_in, inv_ref)
+
+    def third(groups, turned):
+        for i, g in enumerate(groups):
+            terms = []
+            for m in range(COLS):
+                re, im = parts_of(turned, m)
+                if m > 0:
+                    c, s = small_ref[TWIDDLE, m : m + 1, :], small_ref[TWIDDLE + 1, m : m + 1, :]
+                    re, im = re * c - im * s, im * c + re * s
+                terms.append((re, im))
+            for c, (re, im) in enumerate(dft16(terms, -1)):
+                store(g, c, re, im)
+            if finish is not None:
+                finish(g)
+
     for g in range(GROUPS):
-        out = dft16([load(g, c) for c in range(COLS)], 1)
-        for m in range(1, COLS):
-            re, im = out[m]
-            c, s = small_ref[forward, m : m + 1, :], small_ref[forward + 1, m : m + 1, :]
-            out[m] = (re * c + im * s, im * c - re * s)
-        re_in.append([v[0] for v in out])
-        im_in.append([v[1] for v in out])
-    spectrum = matrix_stage(re_in, im_in, fwd_ref)
-    phases = row_phases(first_row, small_ref[WAVENUM], small_ref[STEP8 : STEP8 + 2], sign)
-    re_in, im_in = [[None] * COLS for _ in range(GROUPS)], [[None] * COLS for _ in range(GROUPS)]
-    for m in range(COLS):
-        own_re, own_im = rows_ref[0, m], -sign * rows_ref[1, m]
-        for g in range(GROUPS):
-            row_re, row_im = phases[g][0][m : m + 1, :], phases[g][1][m : m + 1, :]
-            f_re, f_im = own_re * row_re - own_im * row_im, own_re * row_im + own_im * row_re
-            re, im = parts_of(spectrum, m, g)
-            re_in[g][m], im_in[g][m] = re * f_re - im * f_im, re * f_im + im * f_re
-    turned = matrix_stage(re_in, im_in, inv_ref)
-    for g in range(GROUPS):
-        terms = []
-        for m in range(COLS):
-            re, im = parts_of(turned, m, g)
-            if m > 0:
-                c, s = small_ref[TWIDDLE, m : m + 1, :], small_ref[TWIDDLE + 1, m : m + 1, :]
-                re, im = re * c - im * s, im * c + re * s
-            terms.append((re, im))
-        for c, (re, im) in enumerate(dft16(terms, -1)):
-            store(g, c, re, im)
-        if finish is not None:
-            finish(g)
-
+        groups = (g,)
+        third(groups, second(groups, first(groups)))
 
 def potential_kernel(wave_hbm, potential_hbm, out_ref, wave_ref, potential_ref, sems):
     half = GRID // 2

time: 51.6 us -> 51.2 us (level)
  no operation moved by 1% of the time
where the time goes in v6:
time: 51.2 us; the launch traced here: 51 us
  blocking collectives  32.8 us (64%)
  starting transfers between devices  8.6 us (17%)
  waiting for transfers between devices  4.29 us (8%)
  Pallas kernels  4.17 us (8%)
  local copies, waits for them, and re-layouts  0.94 us (2%)
    all_to_all x1, blocking collectives, on_device(): chunks = lax.all_to_all(chunks, 'wa', 0, 0, tiled=True)  32.8 us
    ppermute x1, starting transfers between devices, on_device(): beside = lax.ppermute(own, 'gz', outward)  5.39 us
    ppermute x1, waiting for transfers between devices, on_device(): beside = lax.ppermute(own, 'gz', outward)  2.74 us
    ppermute x1, starting transfers between devices, on_device(): near = lax.ppermute(message, 'gz', [(i, i ^ 1) for i in range(8)])  1.92 us
    pallas_call x1, Pallas kernels, on_device(): pl.pallas_call(y_kernel, out_shape=jax.ShapeDtypeStruct((2, 1, ROWS, GRID...  1.58 us
    ppermute x1, waiting for transfers between devices, on_device(): across = lax.ppermute(own, 'gz', inward)  1.54 us
    pallas_call x1, Pallas kernels, on_device(): pl.pallas_call(potential_kernel, out_shape=jax.ShapeDtypeStruct((2, ROWS,...  1.37 us
    ppermute x1, starting transfers between devices, on_device(): across = lax.ppermute(own, 'gz', inward)  1.29 us
  transfers between devices with their start and end apart: 3, of which 2 were waited for; matrix products, arithmetic and copies ran while one was open for 0% of the time, Pallas kernels for 1%

profile of v6, /device:TPU:1, one launch (start us, length us, event | category | flops | bytes accessed | tf_op | source)
XLA Modules:
  0.0 51.0 jit_solution(18223787600272255626)
XLA Ops:
  0.0 1.4 %shard_map.73.own_ref = bf16[2,32,2048]{2,1,0:T(8,128)(2,1)S(1)} custom-call(f32[2,1,32,2048]{3,2,1,0:T(8,128)} %wave_hbm.1, f32[1,32,2048]{2,1,0:T(8,128)} %potential_hbm.1), custom_call_target="tpu_custom_call" | custom-call | tf_op jit(solution)/shard_map/pallas_call | solution.py:322
  1.4 5.4 %collective-permute-start = (bf16[2,32,2048]{2,1,0:T(8,128)(2,1)S(1)}, bf16[2,32,2048]{2,1,0:T(8,128)(2,1)S(1)}, u32[]{:S(2)}, u32[]{:S(2)}) collective-permute-start(bf16[2,32,2048]{2,1,0:T(8,128)(2,1)S(1)} %shard_map.73.own_ref), channel_id=1, source_target_pairs={{2,1},{4,3},{6,5},{1,2},{3,4},{5,6},{10,9},{12,11},{14,13},{9,10},... | collective-permute-start | bytes 786440 | tf_op jit(solution)/shard_map/ppermute | solution.py:336
  6.8 1.3 %collective-permute-start.1 = (bf16[2,32,2048]{2,1,0:T(8,128)(2,1)S(1)}, bf16[2,32,2048]{2,1,0:T(8,128)(2,1)S(1)}, u32[]{:S(2)}, u32[]{:S(2)}) collective-permute-start(bf16[2,32,2048]{2,1,0:T(8,128)(2,1)S(1)} %shard_map.73.own_ref), channel_id=1, source_target_pairs={{0,2},{2,4},{4,6},{3,1},{5,3},{7,5},{8,10},{10,12},{12,14},{11,9},... | collective-permute-start | bytes 786440 | tf_op jit(solution)/shard_map/ppermute | solution.py:337
  8.1 2.7 %collective-permute-done.beside_ref = bf16[2,32,2048]{2,1,0:T(8,128)(2,1)S(1)} collective-permute-done((bf16[2,32,2048]{2,1,0:T(8,128)(2,1)S(1)}, bf16[2,32,2048]{2,1,0:T(8,128)(2,1)S(1)}, u32[]{:S(2)}, u32[]{:S(2)}) %collective-permute-start) | collective-permute-done | bytes 262176 | tf_op jit(solution)/shard_map/ppermute | solution.py:336
  10.8 0.1 shard_map.75
  11.0 1.9 %collective-permute-start.2 = (bf16[2,32,2048]{2,1,0:T(8,128)(2,1)S(1)}, bf16[2,32,2048]{2,1,0:T(8,128)(2,1)S(1)}, u32[]{:S(2)}, u32[]{:S(2)}) collective-permute-start(bf16[2,32,2048]{2,1,0:T(8,128)(2,1)S(1)} %shard_map.75), channel_id=1, source_target_pairs={{0,1},{1,0},{2,3},{3,2},{4,5},{5,4},{6,7},{7,6},{8,9},{9,8},{10,11... | collective-permute-start | bytes 786440 | tf_op jit(solution)/shard_map/ppermute | solution.py:345
  12.9 0.1 pad_maximum_fusion
  13.0 1.5 %collective-permute-done.1.across_ref = bf16[2,32,2048]{2,1,0:T(8,128)(2,1)S(1)} collective-permute-done((bf16[2,32,2048]{2,1,0:T(8,128)(2,1)S(1)}, bf16[2,32,2048]{2,1,0:T(8,128)(2,1)S(1)}, u32[]{:S(2)}, u32[]{:S(2)}) %collective-permute-start.1) | collective-permute-done | bytes 262176 | tf_op jit(solution)/shard_map/ppermute | solution.py:337
  14.5 0.1 broadcast_in_dim.2.scalar_ref
  14.6 0.0 copy-start
  14.6 0.0 copy-start.1
  14.6 0.0 copy-start.3
  14.6 0.0 copy-start.4
  14.6 0.2 shard_map.74.mixed_ref
  14.8 0.0 collective-permute-done.2.near_ref
  14.8 0.7 %copy-done = bf16[512,256]{1,0:T(8,128)(2,1)S(1)} copy-done((bf16[512,256]{1,0:T(8,128)(2,1)S(1)}, bf16[512,256]{1,0:T(8,128)(2,1)}, u32[]{:S(2)}) %copy-start) | copy-done | bytes 262168
  15.6 0.0 copy-done.1
  15.6 0.1 copy-done.3
  15.7 0.0 copy-done.4
  15.7 0.9 %shard_map.76 = bf16[64,16,128]{2,1,0:T(8,128)(2,1)S(1)} custom-call(f32[2,128]{1,0:T(2,128)S(1)} %broadcast_in_dim.2.scalar_ref, f32[2,32,2048]{2,1,0:T(8,128)S(1)} %shard_map.74.mixed_ref, bf16[2,32,2048]{2,1,0:T(8,128)(2,1)S(1)} %collective-permute-done.2.near_ref, bf16[512,256]{1,0:T(8,128)(2,1)S(1)} %copy-done.3, bf16[512,256]{1,0:T(8,128)(2,1)S(1)} %copy-done, ...), custom_call_target="tpu_custom_call" | custom-call | tf_op jit(solution)/shard_map/pallas_call | solution.py:353
  16.6 0.0 copy-start.2
  16.6 32.8 %all_to_all.5.in_ref = bf16[64,16,128]{2,1,0:T(8,128)(2,1)S(1)} all-to-all(bf16[64,16,128]{2,1,0:T(8,128)(2,1)S(1)} %shard_map.76), channel_id=1, replica_groups=mesh['wa'=64,'gz'=8] {'wa'}, dimensions={0} | all-to-all | bytes 524288 | tf_op jit(solution)/shard_map/all_to_all | solution.py:363
  49.4 0.0 copy-done.2
  49.4 1.6 %shard_map.77 = f32[2,1,32,2048]{3,2,1,0:T(8,128)} custom-call(f32[2,128]{1,0:T(2,128)S(1)} %broadcast_in_dim.2.scalar_ref, bf16[64,16,128]{2,1,0:T(8,128)(2,1)S(1)} %all_to_all.5.in_ref, bf16[512,256]{1,0:T(8,128)(2,1)S(1)} %copy-done.2, bf16[512,256]{1,0:T(8,128)(2,1)S(1)} %copy-done, f32[7,16,128]{2,1,0:T(8,128)S(1)} %copy-done.4, ...), custom_call_target="tpu_custom_call" | custom-call | tf_op jit(solution)/shard_map/pallas_call | solution.py:364
Async XLA Ops:
  1.4 9.4 %collective-permute-start = (bf16[2,32,2048]{2,1,0:T(8,128)(2,1)S(1)}, bf16[2,32,2048]{2,1,0:T(8,128)(2,1)S(1)}, u32[]{:S(2)}, u32[]{:S(2)}) collective-permute-start(bf16[2,32,2048]{2,1,0:T(8,128)(2,1)S(1)} %shard_map.73.own_ref), channel_id=1, source_target_pairs={{2,1},{4,3},{6,5},{1,2},{3,4},{5,6},{10,9},{12,11},{14,13},{9,10},... | collective-permute-start | bytes 786440 | tf_op jit(solution)/shard_map/ppermute | solution.py:336
  6.8 7.8 %collective-permute-start.1 = (bf16[2,32,2048]{2,1,0:T(8,128)(2,1)S(1)}, bf16[2,32,2048]{2,1,0:T(8,128)(2,1)S(1)}, u32[]{:S(2)}, u32[]{:S(2)}) collective-permute-start(bf16[2,32,2048]{2,1,0:T(8,128)(2,1)S(1)} %shard_map.73.own_ref), channel_id=1, source_target_pairs={{0,2},{2,4},{4,6},{3,1},{5,3},{7,5},{8,10},{10,12},{12,14},{11,9},... | collective-permute-start | bytes 786440 | tf_op jit(solution)/shard_map/ppermute | solution.py:337
  11.0 3.9 %collective-permute-start.2 = (bf16[2,32,2048]{2,1,0:T(8,128)(2,1)S(1)}, bf16[2,32,2048]{2,1,0:T(8,128)(2,1)S(1)}, u32[]{:S(2)}, u32[]{:S(2)}) collective-permute-start(bf16[2,32,2048]{2,1,0:T(8,128)(2,1)S(1)} %shard_map.75), channel_id=1, source_target_pairs={{0,1},{1,0},{2,3},{3,2},{4,5},{5,4},{6,7},{7,6},{8,9},{9,8},{10,11... | collective-permute-start | bytes 786440 | tf_op jit(solution)/shard_map/ppermute | solution.py:345
  14.6 1.0 %copy-start = (bf16[512,256]{1,0:T(8,128)(2,1)S(1)}, bf16[512,256]{1,0:T(8,128)(2,1)}, u32[]{:S(2)}) copy-start(bf16[512,256]{1,0:T(8,128)(2,1)} %constant.35.clone.inv_ref) | copy-start | bytes 786436
  14.6 1.0 %copy-start.1 = (f32[2,16,8,128]{3,2,1,0:T(8,128)S(1)}, f32[2,16,8,128]{3,2,1,0:T(8,128)}, u32[]{:S(2)}) copy-start(f32[2,16,8,128]{3,2,1,0:T(8,128)} %constant.37.clone.rows_ref) | copy-start | bytes 393220
  14.6 1.1 %copy-start.3 = (bf16[512,256]{1,0:T(8,128)(2,1)S(1)}, bf16[512,256]{1,0:T(8,128)(2,1)}, u32[]{:S(2)}) copy-start(bf16[512,256]{1,0:T(8,128)(2,1)} %constant.34.clone.fwd_ref) | copy-start | bytes 786436
  14.6 1.1 %copy-start.4 = (f32[7,16,128]{2,1,0:T(8,128)S(1)}, f32[7,16,128]{2,1,0:T(8,128)}, u32[]{:S(2)}) copy-start(f32[7,16,128]{2,1,0:T(8,128)} %constant.36.clone.small_ref) | copy-start | bytes 172036
  16.6 32.8 %copy-start.2 = (bf16[512,256]{1,0:T(8,128)(2,1)S(1)}, bf16[512,256]{1,0:T(8,128)(2,1)}, u32[]{:S(2)}) copy-start(bf16[512,256]{1,0:T(8,128)(2,1)} %constant.38.clone.fwd_ref) | copy-start | bytes 786436

commit v7 on v6

--- a/solution.py
+++ b/solution.py
@@ -239,7 +239,8 @@
     out_ref[1] = (NEAR[0] * im + NEAR[1] * re + FAR * bim).astype(jnp.bfloat16)
 
 
-def mix_kernel(scalar_ref, own_ref, beside_ref, across_ref, out_ref):
+def mix_kernel(scalar_ref, own_ref, beside_ref, across_ref, *tables_and_out):
+    out_ref = tables_and_out[-1]
     centre = scalar_ref[1:2, :]
     for g in range(2):
         rows = slice(16 * g, 16 * g + 16)
@@ -343,13 +344,14 @@
         compiler_params=PARAMS,
     )(own, beside)
     near = lax.ppermute(message, "gz", [(i, i ^ 1) for i in range(8)])
+    held = [jnp.asarray(t[name]) for name in ("fwd_x", "inv", "small", "own")]
     mixed = pl.pallas_call(
         mix_kernel,
         out_shape=jax.ShapeDtypeStruct((2, ROWS, GRID), f32),
-        in_specs=[VMEM] * 4,
+        in_specs=[VMEM] * 8,
         out_specs=VMEM,
         compiler_params=PARAMS,
-    )(scalars, own, beside, across)
+    )(scalars, own, beside, across, *held)
     chunks = pl.pallas_call(
         x_kernel,
         out_shape=jax.ShapeDtypeStruct((PARTS_WA, 16, LANES), bf16),
@@ -359,7 +361,7 @@
             pltpu.VMEM((COLS, 2, ROWS, LANES), f32),
         ],
         compiler_params=PARAMS,
-    )(scalars, mixed, near, t["fwd_x"], t["inv"], t["small"], t["own"])
+    )(scalars, mixed, near, *held)
     chunks = lax.all_to_all(chunks, "wa", 0, 0, tiled=True)
     return pl.pallas_call(
         y_kernel,
@@ -372,7 +374,7 @@
             pltpu.SemaphoreType.DMA((GROUPS, 2)),
         ],
         compiler_params=PARAMS,
-    )(scalars, chunks, t["fwd_y"], t["inv"], t["small"], t["own"])
+    )(scalars, chunks, jnp.asarray(t["fwd_y"]), *held[1:])
 
 
 def solution(mesh):

time: 51.2 us -> 50.9 us (level); the launches traced: 51 us -> 50.1 us
  local copies, waits for them, and re-layouts: 0.94 us -> 0.1 us
    unnamed x10, local copies, waits for them, and re-layouts: 0.88 us -> 0.03 us
where the time goes in v7:
time: 50.9 us; the launch traced here: 50.1 us
  blocking collectives  32.6 us (64%)
  starting transfers between devices  8.73 us (17%)
  waiting for transfers between devices  4.29 us (8%)
  Pallas kernels  4.11 us (8%)
    all_to_all x1, blocking collectives, on_device(): chunks = lax.all_to_all(chunks, 'wa', 0, 0, tiled=True)  32.6 us
    ppermute x1, starting transfers between devices, on_device(): beside = lax.ppermute(own, 'gz', outward)  5.52 us
    ppermute x1, waiting for transfers between devices, on_device(): beside = lax.ppermute(own, 'gz', outward)  2.74 us
    ppermute x1, starting transfers between devices, on_device(): near = lax.ppermute(message, 'gz', [(i, i ^ 1) for i in range(8)])  1.92 us
    ppermute x1, waiting for transfers between devices, on_device(): across = lax.ppermute(own, 'gz', inward)  1.54 us
    pallas_call x1, Pallas kernels, on_device(): pl.pallas_call(y_kernel, out_shape=jax.ShapeDtypeStruct((2, 1, ROWS, GRID...  1.54 us
    pallas_call x1, Pallas kernels, on_device(): pl.pallas_call(potential_kernel, out_shape=jax.ShapeDtypeStruct((2, ROWS,...  1.37 us
    ppermute x1, starting transfers between devices, on_device(): across = lax.ppermute(own, 'gz', inward)  1.29 us
  transfers between devices with their start and end apart: 3, of which 2 were waited for; matrix products, arithmetic and copies ran while one was open for 0% of the time, Pallas kernels for 1%

profile of v7, /device:TPU:1, one launch (start us, length us, event | category | flops | bytes accessed | tf_op | source)
XLA Modules:
  0.0 50.1 jit_solution(18236061356491084338)
XLA Ops:
  0.0 1.4 %shard_map.73.own_ref = bf16[2,32,2048]{2,1,0:T(8,128)(2,1)S(1)} custom-call(f32[2,1,32,2048]{3,2,1,0:T(8,128)} %wave_hbm.1, f32[1,32,2048]{2,1,0:T(8,128)} %potential_hbm.1), custom_call_target="tpu_custom_call" | custom-call | tf_op jit(solution)/shard_map/pallas_call | solution.py:323
  1.4 0.0 copy-start
  1.4 0.0 copy-start.1
  1.4 0.0 copy-start.2
  1.4 5.5 %collective-permute-start = (bf16[2,32,2048]{2,1,0:T(8,128)(2,1)S(1)}, bf16[2,32,2048]{2,1,0:T(8,128)(2,1)S(1)}, u32[]{:S(2)}, u32[]{:S(2)}) collective-permute-start(bf16[2,32,2048]{2,1,0:T(8,128)(2,1)S(1)} %shard_map.73.own_ref), channel_id=1, source_target_pairs={{2,1},{4,3},{6,5},{1,2},{3,4},{5,6},{10,9},{12,11},{14,13},{9,10},... | collective-permute-start | bytes 786440 | tf_op jit(solution)/shard_map/ppermute | solution.py:337
  6.9 1.3 %collective-permute-start.1 = (bf16[2,32,2048]{2,1,0:T(8,128)(2,1)S(1)}, bf16[2,32,2048]{2,1,0:T(8,128)(2,1)S(1)}, u32[]{:S(2)}, u32[]{:S(2)}) collective-permute-start(bf16[2,32,2048]{2,1,0:T(8,128)(2,1)S(1)} %shard_map.73.own_ref), channel_id=1, source_target_pairs={{0,2},{2,4},{4,6},{3,1},{5,3},{7,5},{8,10},{10,12},{12,14},{11,9},... | collective-permute-start | bytes 786440 | tf_op jit(solution)/shard_map/ppermute | solution.py:338
  8.2 2.7 %collective-permute-done.beside_ref = bf16[2,32,2048]{2,1,0:T(8,128)(2,1)S(1)} collective-permute-done((bf16[2,32,2048]{2,1,0:T(8,128)(2,1)S(1)}, bf16[2,32,2048]{2,1,0:T(8,128)(2,1)S(1)}, u32[]{:S(2)}, u32[]{:S(2)}) %collective-permute-start) | collective-permute-done | bytes 262176 | tf_op jit(solution)/shard_map/ppermute | solution.py:337
  11.0 0.0 copy-start.3
  11.0 0.1 shard_map.75
  11.1 1.9 %collective-permute-start.2 = (bf16[2,32,2048]{2,1,0:T(8,128)(2,1)S(1)}, bf16[2,32,2048]{2,1,0:T(8,128)(2,1)S(1)}, u32[]{:S(2)}, u32[]{:S(2)}) collective-permute-start(bf16[2,32,2048]{2,1,0:T(8,128)(2,1)S(1)} %shard_map.75), channel_id=1, source_target_pairs={{0,1},{1,0},{2,3},{3,2},{4,5},{5,4},{6,7},{7,6},{8,9},{9,8},{10,11... | collective-permute-start | bytes 786440 | tf_op jit(solution)/shard_map/ppermute | solution.py:346
  13.1 0.1 pad_maximum_fusion
  13.2 1.5 %collective-permute-done.1.across_ref = bf16[2,32,2048]{2,1,0:T(8,128)(2,1)S(1)} collective-permute-done((bf16[2,32,2048]{2,1,0:T(8,128)(2,1)S(1)}, bf16[2,32,2048]{2,1,0:T(8,128)(2,1)S(1)}, u32[]{:S(2)}, u32[]{:S(2)}) %collective-permute-start.1) | collective-permute-done | bytes 262176 | tf_op jit(solution)/shard_map/ppermute | solution.py:338
  14.7 0.1 broadcast_in_dim.2.scalar_ref
  14.8 0.0 copy-done
  14.8 0.0 copy-done.1
  14.8 0.0 copy-done.2
  14.8 0.0 copy-done.3
  14.8 0.2 shard_map.74.mixed_ref
  15.0 0.0 collective-permute-done.2.near_ref
  15.0 0.8 %shard_map.76 = bf16[64,16,128]{2,1,0:T(8,128)(2,1)S(1)} custom-call(f32[2,128]{1,0:T(2,128)S(1)} %broadcast_in_dim.2.scalar_ref, f32[2,32,2048]{2,1,0:T(8,128)S(1)} %shard_map.74.mixed_ref, bf16[2,32,2048]{2,1,0:T(8,128)(2,1)S(1)} %collective-permute-done.2.near_ref, bf16[512,256]{1,0:T(8,128)(2,1)S(1)} %copy-done.2, bf16[512,256]{1,0:T(8,128)(2,1)S(1)} %copy-done, ...), custom_call_target="tpu_custom_call" | custom-call | tf_op jit(solution)/shard_map/pallas_call | solution.py:355
  15.9 0.0 copy-start.4
  15.9 32.6 %all_to_all.5.in_ref = bf16[64,16,128]{2,1,0:T(8,128)(2,1)S(1)} all-to-all(bf16[64,16,128]{2,1,0:T(8,128)(2,1)S(1)} %shard_map.76), channel_id=1, replica_groups=mesh['wa'=64,'gz'=8] {'wa'}, dimensions={0} | all-to-all | bytes 524288 | tf_op jit(solution)/shard_map/all_to_all | solution.py:365
  48.5 0.0 copy-done.4
  48.5 1.5 %shard_map.77 = f32[2,1,32,2048]{3,2,1,0:T(8,128)} custom-call(f32[2,128]{1,0:T(2,128)S(1)} %broadcast_in_dim.2.scalar_ref, bf16[64,16,128]{2,1,0:T(8,128)(2,1)S(1)} %all_to_all.5.in_ref, bf16[512,256]{1,0:T(8,128)(2,1)S(1)} %copy-done.4, bf16[512,256]{1,0:T(8,128)(2,1)S(1)} %copy-done, f32[7,16,128]{2,1,0:T(8,128)S(1)} %copy-done.3, ...), custom_call_target="tpu_custom_call" | custom-call | tf_op jit(solution)/shard_map/pallas_call | solution.py:366
Async XLA Ops:
  1.4 13.4 %copy-start = (bf16[512,256]{1,0:T(8,128)(2,1)S(1)}, bf16[512,256]{1,0:T(8,128)(2,1)}, u32[]{:S(2)}) copy-start(bf16[512,256]{1,0:T(8,128)(2,1)} %constant.35.clone.tables_and_out_1_.inv_ref) | copy-start | bytes 786436
  1.4 13.4 %copy-start.1 = (f32[2,16,8,128]{3,2,1,0:T(8,128)S(1)}, f32[2,16,8,128]{3,2,1,0:T(8,128)}, u32[]{:S(2)}) copy-start(f32[2,16,8,128]{3,2,1,0:T(8,128)} %constant.37.clone.tables_and_out_3_.rows_ref) | copy-start | bytes 393220
  1.4 13.4 %copy-start.2 = (bf16[512,256]{1,0:T(8,128)(2,1)S(1)}, bf16[512,256]{1,0:T(8,128)(2,1)}, u32[]{:S(2)}) copy-start(bf16[512,256]{1,0:T(8,128)(2,1)} %constant.34.clone.tables_and_out_0_.fwd_ref) | copy-start | bytes 786436
  1.4 9.6 %collective-permute-start = (bf16[2,32,2048]{2,1,0:T(8,128)(2,1)S(1)}, bf16[2,32,2048]{2,1,0:T(8,128)(2,1)S(1)}, u32[]{:S(2)}, u32[]{:S(2)}) collective-permute-start(bf16[2,32,2048]{2,1,0:T(8,128)(2,1)S(1)} %shard_map.73.own_ref), channel_id=1, source_target_pairs={{2,1},{4,3},{6,5},{1,2},{3,4},{5,6},{10,9},{12,11},{14,13},{9,10},... | collective-permute-start | bytes 786440 | tf_op jit(solution)/shard_map/ppermute | solution.py:337
  6.9 7.8 %collective-permute-start.1 = (bf16[2,32,2048]{2,1,0:T(8,128)(2,1)S(1)}, bf16[2,32,2048]{2,1,0:T(8,128)(2,1)S(1)}, u32[]{:S(2)}, u32[]{:S(2)}) collective-permute-start(bf16[2,32,2048]{2,1,0:T(8,128)(2,1)S(1)} %shard_map.73.own_ref), channel_id=1, source_target_pairs={{0,2},{2,4},{4,6},{3,1},{5,3},{7,5},{8,10},{10,12},{12,14},{11,9},... | collective-permute-start | bytes 786440 | tf_op jit(solution)/shard_map/ppermute | solution.py:338
  11.0 3.8 %copy-start.3 = (f32[7,16,128]{2,1,0:T(8,128)S(1)}, f32[7,16,128]{2,1,0:T(8,128)}, u32[]{:S(2)}) copy-start(f32[7,16,128]{2,1,0:T(8,128)} %constant.36.clone.tables_and_out_2_.small_ref) | copy-start | bytes 172036
  11.1 3.9 %collective-permute-start.2 = (bf16[2,32,2048]{2,1,0:T(8,128)(2,1)S(1)}, bf16[2,32,2048]{2,1,0:T(8,128)(2,1)S(1)}, u32[]{:S(2)}, u32[]{:S(2)}) collective-permute-start(bf16[2,32,2048]{2,1,0:T(8,128)(2,1)S(1)} %shard_map.75), channel_id=1, source_target_pairs={{0,1},{1,0},{2,3},{3,2},{4,5},{5,4},{6,7},{7,6},{8,9},{9,8},{10,11... | collective-permute-start | bytes 786440 | tf_op jit(solution)/shard_map/ppermute | solution.py:346
  15.9 32.7 %copy-start.4 = (bf16[512,256]{1,0:T(8,128)(2,1)S(1)}, bf16[512,256]{1,0:T(8,128)(2,1)}, u32[]{:S(2)}) copy-start(bf16[512,256]{1,0:T(8,128)(2,1)} %constant.38.clone.fwd_ref) | copy-start | bytes 786436

commit v8 on v7

--- a/solution.py
+++ b/solution.py
@@ -298,9 +298,8 @@
 
     def send(g):
         rows = slice(8 * g, 8 * g + 8)
-        for p in range(2):
-            copies.append(pltpu.make_async_copy(out_ref.at[p, rows], out_hbm.at[p, 0, rows], sems.at[g, p]))
-            copies[-1].start()
+        copies.append(pltpu.make_async_copy(out_ref.at[:, rows], out_hbm.at[:, 0, rows], sems.at[g]))
+        copies[-1].start()
 
     sweep(load, store, scalar_ref[0:1, :], fwd_ref, inv_ref, small_ref, rows_ref, TWIDDLE_TURNED, -1.0, send)
     for copy in copies:
@@ -371,7 +370,7 @@
         scratch_shapes=[
             pltpu.VMEM((2, ROWS, GRID), f32),
             pltpu.VMEM((2, ROWS, GRID), f32),
-            pltpu.SemaphoreType.DMA((GROUPS, 2)),
+            pltpu.SemaphoreType.DMA((GROUPS,)),
         ],
         compiler_params=PARAMS,
     )(scalars, chunks, jnp.asarray(t["fwd_y"]), *held[1:])

time: 50.9 us -> 50.9 us (level)
  no operation moved by 1% of the time
where the time goes in v8:
time: 50.9 us; the launch traced here: 50 us
  blocking collectives  32.6 us (64%)
  starting transfers between devices  8.73 us (17%)
  waiting for transfers between devices  4.29 us (8%)
  Pallas kernels  4.08 us (8%)
    all_to_all x1, blocking collectives, on_device(): chunks = lax.all_to_all(chunks, 'wa', 0, 0, tiled=True)  32.6 us
    ppermute x1, starting transfers between devices, on_device(): beside = lax.ppermute(own, 'gz', outward)  5.52 us
    ppermute x1, waiting for transfers between devices, on_device(): beside = lax.ppermute(own, 'gz', outward)  2.74 us
    ppermute x1, starting transfers between devices, on_device(): near = lax.ppermute(message, 'gz', [(i, i ^ 1) for i in range(8)])  1.92 us
    ppermute x1, waiting for transfers between devices, on_device(): across = lax.ppermute(own, 'gz', inward)  1.54 us
    pallas_call x1, Pallas kernels, on_device(): pl.pallas_call(y_kernel, out_shape=jax.ShapeDtypeStruct((2, 1, ROWS, GRID...  1.51 us
    pallas_call x1, Pallas kernels, on_device(): pl.pallas_call(potential_kernel, out_shape=jax.ShapeDtypeStruct((2, ROWS,...  1.37 us
    ppermute x1, starting transfers between devices, on_device(): across = lax.ppermute(own, 'gz', inward)  1.29 us
  transfers between devices with their start and end apart: 3, of which 2 were waited for; matrix products, arithmetic and copies ran while one was open for 0% of the time, Pallas kernels for 1%

profile of v8, /device:TPU:1, one launch (start us, length us, event | category | flops | bytes accessed | tf_op | source)
XLA Modules:
  0.0 50.0 jit_solution(17066161577805969025)
XLA Ops:
  0.0 1.4 %shard_map.73.own_ref = bf16[2,32,2048]{2,1,0:T(8,128)(2,1)S(1)} custom-call(f32[2,1,32,2048]{3,2,1,0:T(8,128)} %wave_hbm.1, f32[1,32,2048]{2,1,0:T(8,128)} %potential_hbm.1), custom_call_target="tpu_custom_call" | custom-call | tf_op jit(solution)/shard_map/pallas_call | solution.py:322
  1.4 0.0 copy-start
  1.4 0.0 copy-start.1
  1.4 0.0 copy-start.2
  1.4 5.5 %collective-permute-start = (bf16[2,32,2048]{2,1,0:T(8,128)(2,1)S(1)}, bf16[2,32,2048]{2,1,0:T(8,128)(2,1)S(1)}, u32[]{:S(2)}, u32[]{:S(2)}) collective-permute-start(bf16[2,32,2048]{2,1,0:T(8,128)(2,1)S(1)} %shard_map.73.own_ref), channel_id=1, source_target_pairs={{2,1},{4,3},{6,5},{1,2},{3,4},{5,6},{10,9},{12,11},{14,13},{9,10},... | collective-permute-start | bytes 786440 | tf_op jit(solution)/shard_map/ppermute | solution.py:336
  6.9 1.3 %collective-permute-start.1 = (bf16[2,32,2048]{2,1,0:T(8,128)(2,1)S(1)}, bf16[2,32,2048]{2,1,0:T(8,128)(2,1)S(1)}, u32[]{:S(2)}, u32[]{:S(2)}) collective-permute-start(bf16[2,32,2048]{2,1,0:T(8,128)(2,1)S(1)} %shard_map.73.own_ref), channel_id=1, source_target_pairs={{0,2},{2,4},{4,6},{3,1},{5,3},{7,5},{8,10},{10,12},{12,14},{11,9},... | collective-permute-start | bytes 786440 | tf_op jit(solution)/shard_map/ppermute | solution.py:337
  8.2 2.7 %collective-permute-done.beside_ref = bf16[2,32,2048]{2,1,0:T(8,128)(2,1)S(1)} collective-permute-done((bf16[2,32,2048]{2,1,0:T(8,128)(2,1)S(1)}, bf16[2,32,2048]{2,1,0:T(8,128)(2,1)S(1)}, u32[]{:S(2)}, u32[]{:S(2)}) %collective-permute-start) | collective-permute-done | bytes 262176 | tf_op jit(solution)/shard_map/ppermute | solution.py:336
  11.0 0.0 copy-start.3
  11.0 0.1 shard_map.75
  11.1 1.9 %collective-permute-start.2 = (bf16[2,32,2048]{2,1,0:T(8,128)(2,1)S(1)}, bf16[2,32,2048]{2,1,0:T(8,128)(2,1)S(1)}, u32[]{:S(2)}, u32[]{:S(2)}) collective-permute-start(bf16[2,32,2048]{2,1,0:T(8,128)(2,1)S(1)} %shard_map.75), channel_id=1, source_target_pairs={{0,1},{1,0},{2,3},{3,2},{4,5},{5,4},{6,7},{7,6},{8,9},{9,8},{10,11... | collective-permute-start | bytes 786440 | tf_op jit(solution)/shard_map/ppermute | solution.py:345
  13.1 0.1 pad_maximum_fusion
  13.2 1.5 %collective-permute-done.1.across_ref = bf16[2,32,2048]{2,1,0:T(8,128)(2,1)S(1)} collective-permute-done((bf16[2,32,2048]{2,1,0:T(8,128)(2,1)S(1)}, bf16[2,32,2048]{2,1,0:T(8,128)(2,1)S(1)}, u32[]{:S(2)}, u32[]{:S(2)}) %collective-permute-start.1) | collective-permute-done | bytes 262176 | tf_op jit(solution)/shard_map/ppermute | solution.py:337
  14.7 0.1 broadcast_in_dim.2.scalar_ref
  14.8 0.0 copy-done
  14.8 0.0 copy-done.1
  14.8 0.0 copy-done.2
  14.8 0.0 copy-done.3
  14.8 0.2 shard_map.74.mixed_ref
  15.0 0.0 collective-permute-done.2.near_ref
  15.0 0.8 %shard_map.76 = bf16[64,16,128]{2,1,0:T(8,128)(2,1)S(1)} custom-call(f32[2,128]{1,0:T(2,128)S(1)} %broadcast_in_dim.2.scalar_ref, f32[2,32,2048]{2,1,0:T(8,128)S(1)} %shard_map.74.mixed_ref, bf16[2,32,2048]{2,1,0:T(8,128)(2,1)S(1)} %collective-permute-done.2.near_ref, bf16[512,256]{1,0:T(8,128)(2,1)S(1)} %copy-done.2, bf16[512,256]{1,0:T(8,128)(2,1)S(1)} %copy-done, ...), custom_call_target="tpu_custom_call" | custom-call | tf_op jit(solution)/shard_map/pallas_call | solution.py:354
  15.9 0.0 copy-start.4
  15.9 32.6 %all_to_all.5.in_ref = bf16[64,16,128]{2,1,0:T(8,128)(2,1)S(1)} all-to-all(bf16[64,16,128]{2,1,0:T(8,128)(2,1)S(1)} %shard_map.76), channel_id=1, replica_groups=mesh['wa'=64,'gz'=8] {'wa'}, dimensions={0} | all-to-all | bytes 524288 | tf_op jit(solution)/shard_map/all_to_all | solution.py:364
  48.5 0.0 copy-done.4
  48.5 1.5 %shard_map.77 = f32[2,1,32,2048]{3,2,1,0:T(8,128)} custom-call(f32[2,128]{1,0:T(2,128)S(1)} %broadcast_in_dim.2.scalar_ref, bf16[64,16,128]{2,1,0:T(8,128)(2,1)S(1)} %all_to_all.5.in_ref, bf16[512,256]{1,0:T(8,128)(2,1)S(1)} %copy-done.4, bf16[512,256]{1,0:T(8,128)(2,1)S(1)} %copy-done, f32[7,16,128]{2,1,0:T(8,128)S(1)} %copy-done.3, ...), custom_call_target="tpu_custom_call" | custom-call | tf_op jit(solution)/shard_map/pallas_call | solution.py:365
Async XLA Ops:
  1.4 13.4 %copy-start = (bf16[512,256]{1,0:T(8,128)(2,1)S(1)}, bf16[512,256]{1,0:T(8,128)(2,1)}, u32[]{:S(2)}) copy-start(bf16[512,256]{1,0:T(8,128)(2,1)} %constant.35.clone.tables_and_out_1_.inv_ref) | copy-start | bytes 786436
  1.4 13.4 %copy-start.1 = (f32[2,16,8,128]{3,2,1,0:T(8,128)S(1)}, f32[2,16,8,128]{3,2,1,0:T(8,128)}, u32[]{:S(2)}) copy-start(f32[2,16,8,128]{3,2,1,0:T(8,128)} %constant.37.clone.tables_and_out_3_.rows_ref) | copy-start | bytes 393220
  1.4 13.4 %copy-start.2 = (bf16[512,256]{1,0:T(8,128)(2,1)S(1)}, bf16[512,256]{1,0:T(8,128)(2,1)}, u32[]{:S(2)}) copy-start(bf16[512,256]{1,0:T(8,128)(2,1)} %constant.34.clone.tables_and_out_0_.fwd_ref) | copy-start | bytes 786436
  1.4 9.6 %collective-permute-start = (bf16[2,32,2048]{2,1,0:T(8,128)(2,1)S(1)}, bf16[2,32,2048]{2,1,0:T(8,128)(2,1)S(1)}, u32[]{:S(2)}, u32[]{:S(2)}) collective-permute-start(bf16[2,32,2048]{2,1,0:T(8,128)(2,1)S(1)} %shard_map.73.own_ref), channel_id=1, source_target_pairs={{2,1},{4,3},{6,5},{1,2},{3,4},{5,6},{10,9},{12,11},{14,13},{9,10},... | collective-permute-start | bytes 786440 | tf_op jit(solution)/shard_map/ppermute | solution.py:336
  6.9 7.8 %collective-permute-start.1 = (bf16[2,32,2048]{2,1,0:T(8,128)(2,1)S(1)}, bf16[2,32,2048]{2,1,0:T(8,128)(2,1)S(1)}, u32[]{:S(2)}, u32[]{:S(2)}) collective-permute-start(bf16[2,32,2048]{2,1,0:T(8,128)(2,1)S(1)} %shard_map.73.own_ref), channel_id=1, source_target_pairs={{0,2},{2,4},{4,6},{3,1},{5,3},{7,5},{8,10},{10,12},{12,14},{11,9},... | collective-permute-start | bytes 786440 | tf_op jit(solution)/shard_map/ppermute | solution.py:337
  11.0 3.8 %copy-start.3 = (f32[7,16,128]{2,1,0:T(8,128)S(1)}, f32[7,16,128]{2,1,0:T(8,128)}, u32[]{:S(2)}) copy-start(f32[7,16,128]{2,1,0:T(8,128)} %constant.36.clone.tables_and_out_2_.small_ref) | copy-start | bytes 172036
  11.1 3.9 %collective-permute-start.2 = (bf16[2,32,2048]{2,1,0:T(8,128)(2,1)S(1)}, bf16[2,32,2048]{2,1,0:T(8,128)(2,1)S(1)}, u32[]{:S(2)}, u32[]{:S(2)}) collective-permute-start(bf16[2,32,2048]{2,1,0:T(8,128)(2,1)S(1)} %shard_map.75), channel_id=1, source_target_pairs={{0,1},{1,0},{2,3},{3,2},{4,5},{5,4},{6,7},{7,6},{8,9},{9,8},{10,11... | collective-permute-start | bytes 786440 | tf_op jit(solution)/shard_map/ppermute | solution.py:345
  15.9 32.7 %copy-start.4 = (bf16[512,256]{1,0:T(8,128)(2,1)S(1)}, bf16[512,256]{1,0:T(8,128)(2,1)}, u32[]{:S(2)}) copy-start(bf16[512,256]{1,0:T(8,128)(2,1)} %constant.38.clone.fwd_ref) | copy-start | bytes 786436

commit v9 on v7

--- a/solution.py
+++ b/solution.py
@@ -233,10 +233,13 @@
 
 
 def message_kernel(own_ref, beside_ref, out_ref):
-    re, im = own_ref[0].astype(jnp.float32), own_ref[1].astype(jnp.float32)
-    bre, bim = beside_ref[0].astype(jnp.float32), beside_ref[1].astype(jnp.float32)
-    out_ref[0] = (NEAR[0] * re - NEAR[1] * im + FAR * bre).astype(jnp.bfloat16)
-    out_ref[1] = (NEAR[0] * im + NEAR[1] * re + FAR * bim).astype(jnp.bfloat16)
+    for g in range(2):
+        rows = slice(16 * g, 16 * g + 16)
+        for c in range(COLS):
+            at = slice(LANES * c, LANES * c + LANES)
+            re, im, bre, bim = (ref[p, rows, at].astype(jnp.float32) for ref in (own_ref, beside_ref) for p in range(2))
+            out_ref[0, rows, at] = (NEAR[0] * re - NEAR[1] * im + FAR * bre).astype(jnp.bfloat16)
+            out_ref[1, rows, at] = (NEAR[0] * im + NEAR[1] * re + FAR * bim).astype(jnp.bfloat16)
 
 
 def mix_kernel(scalar_ref, own_ref, beside_ref, across_ref, *tables_and_out):

time: 50.9 us -> 50.9 us (level)
  no operation moved by 1% of the time
where the time goes in v9:
time: 50.9 us; the launch traced here: 50.1 us
  blocking collectives  32.6 us (64%)
  starting transfers between devices  8.73 us (17%)
  waiting for transfers between devices  4.29 us (8%)
  Pallas kernels  4.1 us (8%)
    all_to_all x1, blocking collectives, on_device(): chunks = lax.all_to_all(chunks, 'wa', 0, 0, tiled=True)  32.6 us
    ppermute x1, starting transfers between devices, on_device(): beside = lax.ppermute(own, 'gz', outward)  5.52 us
    ppermute x1, waiting for transfers between devices, on_device(): beside = lax.ppermute(own, 'gz', outward)  2.74 us
    ppermute x1, starting transfers between devices, on_device(): near = lax.ppermute(message, 'gz', [(i, i ^ 1) for i in range(8)])  1.92 us
    ppermute x1, waiting for transfers between devices, on_device(): across = lax.ppermute(own, 'gz', inward)  1.55 us
    pallas_call x1, Pallas kernels, on_device(): pl.pallas_call(y_kernel, out_shape=jax.ShapeDtypeStruct((2, 1, ROWS, GRID...  1.54 us
    pallas_call x1, Pallas kernels, on_device(): pl.pallas_call(potential_kernel, out_shape=jax.ShapeDtypeStruct((2, ROWS,...  1.37 us
    ppermute x1, starting transfers between devices, on_device(): across = lax.ppermute(own, 'gz', inward)  1.29 us
  transfers between devices with their start and end apart: 3, of which 2 were waited for; matrix products, arithmetic and copies ran while one was open for 0% of the time, Pallas kernels for 1%

profile of v9, /device:TPU:1, one launch (start us, length us, event | category | flops | bytes accessed | tf_op | source)
XLA Modules:
  0.0 50.1 jit_solution(1691861570400071385)
XLA Ops:
  0.0 1.4 %shard_map.73.own_ref = bf16[2,32,2048]{2,1,0:T(8,128)(2,1)S(1)} custom-call(f32[2,1,32,2048]{3,2,1,0:T(8,128)} %wave_hbm.1, f32[1,32,2048]{2,1,0:T(8,128)} %potential_hbm.1), custom_call_target="tpu_custom_call" | custom-call | tf_op jit(solution)/shard_map/pallas_call | solution.py:326
  1.4 0.0 copy-start
  1.4 0.0 copy-start.1
  1.4 0.0 copy-start.2
  1.4 5.5 %collective-permute-start = (bf16[2,32,2048]{2,1,0:T(8,128)(2,1)S(1)}, bf16[2,32,2048]{2,1,0:T(8,128)(2,1)S(1)}, u32[]{:S(2)}, u32[]{:S(2)}) collective-permute-start(bf16[2,32,2048]{2,1,0:T(8,128)(2,1)S(1)} %shard_map.73.own_ref), channel_id=1, source_target_pairs={{2,1},{4,3},{6,5},{1,2},{3,4},{5,6},{10,9},{12,11},{14,13},{9,10},... | collective-permute-start | bytes 786440 | tf_op jit(solution)/shard_map/ppermute | solution.py:340
  6.9 1.3 %collective-permute-start.1 = (bf16[2,32,2048]{2,1,0:T(8,128)(2,1)S(1)}, bf16[2,32,2048]{2,1,0:T(8,128)(2,1)S(1)}, u32[]{:S(2)}, u32[]{:S(2)}) collective-permute-start(bf16[2,32,2048]{2,1,0:T(8,128)(2,1)S(1)} %shard_map.73.own_ref), channel_id=1, source_target_pairs={{0,2},{2,4},{4,6},{3,1},{5,3},{7,5},{8,10},{10,12},{12,14},{11,9},... | collective-permute-start | bytes 786440 | tf_op jit(solution)/shard_map/ppermute | solution.py:341
  8.2 2.7 %collective-permute-done.beside_ref = bf16[2,32,2048]{2,1,0:T(8,128)(2,1)S(1)} collective-permute-done((bf16[2,32,2048]{2,1,0:T(8,128)(2,1)S(1)}, bf16[2,32,2048]{2,1,0:T(8,128)(2,1)S(1)}, u32[]{:S(2)}, u32[]{:S(2)}) %collective-permute-start) | collective-permute-done | bytes 262176 | tf_op jit(solution)/shard_map/ppermute | solution.py:340
  11.0 0.0 copy-start.3
  11.0 0.1 shard_map.75
  11.1 1.9 %collective-permute-start.2 = (bf16[2,32,2048]{2,1,0:T(8,128)(2,1)S(1)}, bf16[2,32,2048]{2,1,0:T(8,128)(2,1)S(1)}, u32[]{:S(2)}, u32[]{:S(2)}) collective-permute-start(bf16[2,32,2048]{2,1,0:T(8,128)(2,1)S(1)} %shard_map.75), channel_id=1, source_target_pairs={{0,1},{1,0},{2,3},{3,2},{4,5},{5,4},{6,7},{7,6},{8,9},{9,8},{10,11... | collective-permute-start | bytes 786440 | tf_op jit(solution)/shard_map/ppermute | solution.py:349
  13.1 0.1 pad_maximum_fusion
  13.1 1.6 %collective-permute-done.1.across_ref = bf16[2,32,2048]{2,1,0:T(8,128)(2,1)S(1)} collective-permute-done((bf16[2,32,2048]{2,1,0:T(8,128)(2,1)S(1)}, bf16[2,32,2048]{2,1,0:T(8,128)(2,1)S(1)}, u32[]{:S(2)}, u32[]{:S(2)}) %collective-permute-start.1) | collective-permute-done | bytes 262176 | tf_op jit(solution)/shard_map/ppermute | solution.py:341
  14.7 0.1 broadcast_in_dim.2.scalar_ref
  14.8 0.0 copy-done
  14.8 0.0 copy-done.1
  14.8 0.0 copy-done.2
  14.8 0.0 copy-done.3
  14.8 0.2 shard_map.74.mixed_ref
  15.0 0.0 collective-permute-done.2.near_ref
  15.0 0.8 %shard_map.76 = bf16[64,16,128]{2,1,0:T(8,128)(2,1)S(1)} custom-call(f32[2,128]{1,0:T(2,128)S(1)} %broadcast_in_dim.2.scalar_ref, f32[2,32,2048]{2,1,0:T(8,128)S(1)} %shard_map.74.mixed_ref, bf16[2,32,2048]{2,1,0:T(8,128)(2,1)S(1)} %collective-permute-done.2.near_ref, bf16[512,256]{1,0:T(8,128)(2,1)S(1)} %copy-done.2, bf16[512,256]{1,0:T(8,128)(2,1)S(1)} %copy-done, ...), custom_call_target="tpu_custom_call" | custom-call | tf_op jit(solution)/shard_map/pallas_call | solution.py:358
  15.9 0.0 copy-start.4
  15.9 32.6 %all_to_all.5.in_ref = bf16[64,16,128]{2,1,0:T(8,128)(2,1)S(1)} all-to-all(bf16[64,16,128]{2,1,0:T(8,128)(2,1)S(1)} %shard_map.76), channel_id=1, replica_groups=mesh['wa'=64,'gz'=8] {'wa'}, dimensions={0} | all-to-all | bytes 524288 | tf_op jit(solution)/shard_map/all_to_all | solution.py:368
  48.5 0.0 copy-done.4
  48.5 1.5 %shard_map.77 = f32[2,1,32,2048]{3,2,1,0:T(8,128)} custom-call(f32[2,128]{1,0:T(2,128)S(1)} %broadcast_in_dim.2.scalar_ref, bf16[64,16,128]{2,1,0:T(8,128)(2,1)S(1)} %all_to_all.5.in_ref, bf16[512,256]{1,0:T(8,128)(2,1)S(1)} %copy-done.4, bf16[512,256]{1,0:T(8,128)(2,1)S(1)} %copy-done, f32[7,16,128]{2,1,0:T(8,128)S(1)} %copy-done.3, ...), custom_call_target="tpu_custom_call" | custom-call | tf_op jit(solution)/shard_map/pallas_call | solution.py:369
Async XLA Ops:
  1.4 13.4 %copy-start = (bf16[512,256]{1,0:T(8,128)(2,1)S(1)}, bf16[512,256]{1,0:T(8,128)(2,1)}, u32[]{:S(2)}) copy-start(bf16[512,256]{1,0:T(8,128)(2,1)} %constant.35.clone.tables_and_out_1_.inv_ref) | copy-start | bytes 786436
  1.4 13.4 %copy-start.1 = (f32[2,16,8,128]{3,2,1,0:T(8,128)S(1)}, f32[2,16,8,128]{3,2,1,0:T(8,128)}, u32[]{:S(2)}) copy-start(f32[2,16,8,128]{3,2,1,0:T(8,128)} %constant.37.clone.tables_and_out_3_.rows_ref) | copy-start | bytes 393220
  1.4 13.4 %copy-start.2 = (bf16[512,256]{1,0:T(8,128)(2,1)S(1)}, bf16[512,256]{1,0:T(8,128)(2,1)}, u32[]{:S(2)}) copy-start(bf16[512,256]{1,0:T(8,128)(2,1)} %constant.34.clone.tables_and_out_0_.fwd_ref) | copy-start | bytes 786436
  1.4 9.6 %collective-permute-start = (bf16[2,32,2048]{2,1,0:T(8,128)(2,1)S(1)}, bf16[2,32,2048]{2,1,0:T(8,128)(2,1)S(1)}, u32[]{:S(2)}, u32[]{:S(2)}) collective-permute-start(bf16[2,32,2048]{2,1,0:T(8,128)(2,1)S(1)} %shard_map.73.own_ref), channel_id=1, source_target_pairs={{2,1},{4,3},{6,5},{1,2},{3,4},{5,6},{10,9},{12,11},{14,13},{9,10},... | collective-permute-start | bytes 786440 | tf_op jit(solution)/shard_map/ppermute | solution.py:340
  6.9 7.8 %collective-permute-start.1 = (bf16[2,32,2048]{2,1,0:T(8,128)(2,1)S(1)}, bf16[2,32,2048]{2,1,0:T(8,128)(2,1)S(1)}, u32[]{:S(2)}, u32[]{:S(2)}) collective-permute-start(bf16[2,32,2048]{2,1,0:T(8,128)(2,1)S(1)} %shard_map.73.own_ref), channel_id=1, source_target_pairs={{0,2},{2,4},{4,6},{3,1},{5,3},{7,5},{8,10},{10,12},{12,14},{11,9},... | collective-permute-start | bytes 786440 | tf_op jit(solution)/shard_map/ppermute | solution.py:341
  11.0 3.8 %copy-start.3 = (f32[7,16,128]{2,1,0:T(8,128)S(1)}, f32[7,16,128]{2,1,0:T(8,128)}, u32[]{:S(2)}) copy-start(f32[7,16,128]{2,1,0:T(8,128)} %constant.36.clone.tables_and_out_2_.small_ref) | copy-start | bytes 172036
  11.1 3.9 %collective-permute-start.2 = (bf16[2,32,2048]{2,1,0:T(8,128)(2,1)S(1)}, bf16[2,32,2048]{2,1,0:T(8,128)(2,1)S(1)}, u32[]{:S(2)}, u32[]{:S(2)}) collective-permute-start(bf16[2,32,2048]{2,1,0:T(8,128)(2,1)S(1)} %shard_map.75), channel_id=1, source_target_pairs={{0,1},{1,0},{2,3},{3,2},{4,5},{5,4},{6,7},{7,6},{8,9},{9,8},{10,11... | collective-permute-start | bytes 786440 | tf_op jit(solution)/shard_map/ppermute | solution.py:349
  15.9 32.6 %copy-start.4 = (bf16[512,256]{1,0:T(8,128)(2,1)S(1)}, bf16[512,256]{1,0:T(8,128)(2,1)}, u32[]{:S(2)}) copy-start(bf16[512,256]{1,0:T(8,128)(2,1)} %constant.38.clone.fwd_ref) | copy-start | bytes 786436
